TPU v7x, 512 devices: a whole 4x8x8 slice. The times are simulated.
512 devices in a mesh: queue: 32 (over z_lo, x, core), dp: 16 (over y, z_hi).
Axes of the slice: x: 4, y: 8, z: 8 (z_hi: 2, z_lo: 4; z = z_hi * 4 + z_lo), core: 2. Of those that a mesh axis runs over, the one named last changes fastest.
Arguments:
- stream: bfloat16 [57344, 1536], P(('queue', 'dp')), may hold values from -6 to 6
- incoming: bfloat16 [1792, 1536], P('dp'), may hold values from -6 to 6
- levels: int32 [2, 32], replicated, may hold values from 0 to 31
- bounds: int32 [512, 2], P(('queue', 'dp')), may hold values from 0 to 512, as said below
- mod_table: float32 [32, 3, 1536], replicated, may hold values from -3 to 3
- w_query: bfloat16 [1536, 1536], P('dp'), may hold values from -0.15625 to 0.15625
- w_key: bfloat16 [1536, 1536], P('dp'), may hold values from -0.15625 to 0.15625
- w_value: bfloat16 [1536, 1536], P('dp'), may hold values from -0.15625 to 0.15625
- gain_query: float32 [1536], replicated, may hold values from 0.5 to 7
- gain_key: float32 [1536], replicated, may hold values from 0.5 to 7
Outputs:
- queue_state: bfloat16 [57344, 1536], P(('queue', 'dp'))
Inputs may be any that keep to these rules, and one draw needn't show every extreme that they name: bounds[f, 0] is f - 1 or f, and bounds[f, 1] is f + 1 or f + 2, clipped to 0 and 512.
All inputs are finite; a program needn't handle non-finite values.
Results may differ from a plain program's by a relative error of at most 0.039.
Values may be sent and summed in bfloat16 or wider, within the bound.
No kernel may reach another device: no remote copies, remote signals or barrier semaphores. Data moves between devices by JAX's collectives and lax.ppermute only.
A program may use at most 64 MiB of HBM per device.

v0:
```python
import jax
import jax.numpy as jnp
from jax import lax
from jax.sharding import PartitionSpec as P

HEADS = 12
HEAD_DIM = 128


epsilon = 1e-06


def extended(cells, sides, width):
    for axis, dim in sides:
        count = lax.axis_size(axis)
        ends = count - 1
        head = lax.slice_in_dim(cells, 0, width, axis=dim)
        tail = lax.slice_in_dim(cells, cells.shape[dim] - width, cells.shape[dim], axis=dim)
        cells = jnp.concatenate(
            [
                lax.ppermute(tail, axis, [(i, (i + 1) % count) for i in range(ends)]),
                cells,
                lax.ppermute(head, axis, [((i + 1) % count, i) for i in range(ends)]),
            ],
            axis=dim,
        )
    return cells


def shifted(block, axis, distance):
    devices = range(lax.axis_size(axis))
    route = [(i - distance, i) for i in devices if i - distance in devices]
    return lax.ppermute(block, axis, route)


def layer_norm(values):
    average = jnp.mean(values, axis=-1, keepdims=True)
    centred = values - average
    spread = jnp.mean(centred * centred, axis=-1, keepdims=True)
    return centred * lax.rsqrt(spread + epsilon)


def rms_norm(values, gain):
    power = jnp.mean(values * values, axis=-1, keepdims=True)
    return values * lax.rsqrt(power + epsilon) * gain


def modulate(stream, level, mod_table):
    selector = jnp.arange(mod_table.shape[0], dtype=jnp.int32) == level
    picked = jnp.sum(jnp.where(selector[:, None, None], mod_table, 0.0), axis=0)
    widened = stream.astype(jnp.float32)
    normed = (layer_norm(widened) * (1.0 + picked[1][None, :]) + picked[0][None, :]).astype(
        jnp.bfloat16
    )
    return (normed, widened, picked[2])


def project(normed, full_query, full_key, full_value):
    return (
        jnp.dot(normed, full_query, preferred_element_type=jnp.float32),
        jnp.dot(normed, full_key, preferred_element_type=jnp.float32),
        jnp.dot(normed, full_value, preferred_element_type=jnp.float32),
    )


def finish(widened, gate_row, projected, gain_query, gain_key, frame, lower, upper):
    tok_rows, model_width = widened.shape
    query = rms_norm(projected[0], gain_query).astype(jnp.bfloat16)
    key_own = rms_norm(projected[1], gain_key).astype(jnp.bfloat16)
    value_own = projected[2].astype(jnp.bfloat16)
    stacked = jnp.stack([key_own, value_own], axis=0)[:, None]
    beside_all = extended(stacked, ((("queue", "dp"), 1),), 1)
    key_block = beside_all[0].reshape(3 * tok_rows, HEADS, HEAD_DIM)
    value_block = beside_all[1].reshape(3 * tok_rows, HEADS, HEAD_DIM)
    query_heads = query.reshape(tok_rows, HEADS, HEAD_DIM)
    scores = jnp.einsum(
        "qhd,khd->hqk", query_heads, key_block, preferred_element_type=jnp.float32
    ) * HEAD_DIM ** (-0.5)
    key_frame = frame - 1 + jnp.arange(3 * tok_rows, dtype=jnp.int32) // tok_rows
    allowed = (key_frame >= lower) & (key_frame < upper)
    scores = jnp.where(allowed[None, None, :], scores, jnp.float32(-1e30))
    peak = jnp.max(scores, axis=-1, keepdims=True)
    weights = jnp.exp(scores - peak)
    total = jnp.sum(weights, axis=-1, keepdims=True)
    probs = (weights / total).astype(jnp.bfloat16)
    attended = jnp.einsum("hqk,khd->qhd", probs, value_block, preferred_element_type=jnp.float32)
    attended = attended.astype(jnp.bfloat16).reshape(tok_rows, model_width)
    return (widened + gate_row[None, :] * attended.astype(jnp.float32)).astype(jnp.bfloat16)


def shards(
    stream, incoming, levels, bounds, mod_table, w_query, w_key, w_value, gain_query, gain_key
):
    section = lax.axis_index("queue")
    frame = section * lax.axis_size("dp") + lax.axis_index("dp")
    lower = bounds[0, 0]
    upper = bounds[0, 1]
    normed_first, widened_first, gate_first = modulate(stream, levels[0, section], mod_table)
    full_query, full_key, full_value = (
        lax.all_gather(w_query, "dp", axis=0, tiled=True),
        lax.all_gather(w_key, "dp", axis=0, tiled=True),
        lax.all_gather(w_value, "dp", axis=0, tiled=True),
    )
    projected_first = project(normed_first, full_query, full_key, full_value)
    first = finish(
        widened_first, gate_first, projected_first, gain_query, gain_key, frame, lower, upper
    )
    moved = shifted(first, "queue", 1)
    entering = jnp.where(section == 0, incoming, moved)
    normed_second, widened_second, gate_second = modulate(entering, levels[1, section], mod_table)
    projected_second = project(normed_second, full_query, full_key, full_value)
    return finish(
        widened_second, gate_second, projected_second, gain_query, gain_key, frame, lower, upper
    )


def solution(mesh):
    in_specs = (
        P(("queue", "dp"), None),
        P("dp", None),
        P(),
        P(("queue", "dp"), None),
        P(),
        P("dp", None),
        P("dp", None),
        P("dp", None),
        P(),
        P(),
    )
    out_specs = P(("queue", "dp"), None)
    return jax.shard_map(shards, mesh=mesh, in_specs=in_specs, out_specs=out_specs, check_vma=False)
```

profile of v0, /device:TPU:1, one launch (start us, length us, event | category | flops | bytes accessed | tf_op | source)
XLA Modules:
  0.0 590.1 jit_solution(1144529018042303966)
XLA Ops:
  15.9 137.1 %all-gather.4.cloned.1.call-done = bf16[1536,1536]{1,0:T(8,128)(2,1)} async-done(((bf16[96,1536]{1,0:T(8,128)(2,1)}), bf16[1536,1536]{1,0:T(8,128)(2,1)}) %all-gather.4.cloned.1.call-update) | async-done | bytes 4718608 | tf_op jit(solution)/shard_map/all_gather | solution.py:101
  152.9 3.7 multiply_reduce_fusion.3
  156.7 133.5 %all-gather.6.cloned.1.call-done = bf16[1536,1536]{1,0:T(8,128)(2,1)} async-done(((bf16[96,1536]{1,0:T(8,128)(2,1)}), bf16[1536,1536]{1,0:T(8,128)(2,1)}) %all-gather.6.cloned.1.call-update) | async-done | bytes 4718608 | tf_op jit(solution)/shard_map/all_gather | solution.py:102
  290.1 3.6 fusion.2
  293.9 1.9 collective-permute-start
  295.9 9.7 %collective-permute-start.1 = (bf16[2,1,112,1536]{3,2,0,1:T(8,128)(2,1)S(1)}, bf16[2,1,112,1536]{3,2,0,1:T(8,128)(2,1)S(1)}, u32[]{:S(2)}, u32[]{:S(2)}) collective-permute-start(bf16[2,1,112,1536]{3,2,0,1:T(8,128)(2,1)S(1)} %maximum_bitcast_fusion), channel_id=1, source_target_pairs={{1,0},{2,1},{3,2},{4,3},{5,4},{6,5},{7,6},{8,7},{9,8},{10,9},{11,1... | collective-permute-start | bytes 2064392 | tf_op jit(solution)/shard_map/ppermute | solution.py:23
  305.5 167.0 %all-gather.8.cloned.1.call-done = bf16[1536,1536]{1,0:T(8,128)(2,1)} async-done(((bf16[96,1536]{1,0:T(8,128)(2,1)}), bf16[1536,1536]{1,0:T(8,128)(2,1)}) %all-gather.8.cloned.1.call-update) | async-done | bytes 4718608 | tf_op jit(solution)/shard_map/all_gather | solution.py:100
  472.5 3.7 multiply_reduce_fusion.2
  477.0 1.6 reshape_squeeze.13
  478.6 1.6 reshape_squeeze.12
  480.2 2.4 fusion.73
  482.6 2.7 fusion.9
  485.9 6.5 %collective-permute-start.2 = (bf16[112,1536]{0,1:T(8,128)(2,1)S(1)}, bf16[112,1536]{0,1:T(8,128)(2,1)S(1)}, u32[]{:S(2)}, u32[]{:S(2)}) collective-permute-start(bf16[112,1536]{0,1:T(8,128)(2,1)S(1)} %fusion.34), channel_id=1, source_target_pairs={{0,16},{16,32},{32,48},{48,64},{64,80},{80,96},{96,112},{112,128},... | collective-permute-start | bytes 1032200 | tf_op jit(solution)/shard_map/ppermute | solution.py:33
  492.7 4.4 collective-permute-done.2
  497.6 3.8 multiply_reduce_fusion.1
  501.6 3.6 fusion.3
  505.3 1.9 collective-permute-start.3
  507.2 9.8 %collective-permute-start.4 = (bf16[2,1,112,1536]{3,2,0,1:T(8,128)(2,1)S(1)}, bf16[2,1,112,1536]{3,2,0,1:T(8,128)(2,1)S(1)}, u32[]{:S(2)}, u32[]{:S(2)}) collective-permute-start(bf16[2,1,112,1536]{3,2,0,1:T(8,128)(2,1)S(1)} %maximum_bitcast_fusion.1), channel_id=1, source_target_pairs={{1,0},{2,1},{3,2},{4,3},{5,4},{6,5},{7,6},{8,7},{9,8},{10,9},{11,1... | collective-permute-start | bytes 2064392 | tf_op jit(solution)/shard_map/ppermute | solution.py:23
  518.8 31.1 %collective-permute-done.3 = bf16[2,1,112,1536]{3,2,0,1:T(8,128)(2,1)S(1)} collective-permute-done((bf16[2,1,112,1536]{3,2,0,1:T(8,128)(2,1)S(1)}, bf16[2,1,112,1536]{3,2,0,1:T(8,128)(2,1)S(1)}, u32[]{:S(2)}, u32[]{:S(2)}) %collective-permute-start.3) | collective-permute-done | bytes 688160 | tf_op jit(solution)/shard_map/ppermute | solution.py:21
  549.9 23.5 %collective-permute-done.4 = bf16[2,1,112,1536]{3,2,0,1:T(8,128)(2,1)S(1)} collective-permute-done((bf16[2,1,112,1536]{3,2,0,1:T(8,128)(2,1)S(1)}, bf16[2,1,112,1536]{3,2,0,1:T(8,128)(2,1)S(1)}, u32[]{:S(2)}, u32[]{:S(2)}) %collective-permute-start.4) | collective-permute-done | bytes 688160 | tf_op jit(solution)/shard_map/ppermute | solution.py:23
  573.8 1.6 reshape_squeeze.15
  575.4 1.6 reshape_squeeze.14
  577.0 2.4 fusion.76
  579.4 2.7 fusion.7
  (64 shorter events, 15.2 us)
Async XLA Ops:
  6.5 8.6 %copy-start.2 = (f32[32,3,1536]{2,0,1:T(8,128)S(1)}, f32[32,3,1536]{2,0,1:T(8,128)}, u32[]{:S(2)}) copy-start(f32[32,3,1536]{2,0,1:T(8,128)} %param.14) | copy-start | bytes 1769476
  6.5 146.4 %all-gather.4.cloned.1.call-start = ((), (), s32[]{:S(2)}) async-start(), calls=%async_computation | async-start | bytes 5013504 | tf_op jit(solution)/shard_map/all_gather | solution.py:101
  7.3 282.9 %all-gather.6.cloned.1.call-start = ((), (), s32[]{:S(2)}) async-start(), calls=%async_computation.1 | async-start | bytes 5013504 | tf_op jit(solution)/shard_map/all_gather | solution.py:102
  8.0 464.5 %all-gather.8.cloned.1.call-start = ((), (), s32[]{:S(2)}) async-start(), calls=%async_computation.2 | async-start | bytes 5013504 | tf_op jit(solution)/shard_map/all_gather | solution.py:100
  156.6 137.1 %copy-start.4 = (f32[1536]{0:T(1024)S(1)}, f32[1536]{0:T(1024)}, u32[]{:S(2)}) copy-start(f32[1536]{0:T(1024)} %param.19) | copy-start | bytes 18436
  293.9 182.3 %copy-start.5 = (f32[1536]{0:T(1024)S(1)}, f32[1536]{0:T(1024)}, u32[]{:S(2)}) copy-start(f32[1536]{0:T(1024)} %param.18) | copy-start | bytes 18436
  293.9 182.7 %collective-permute-start = (bf16[2,1,112,1536]{3,2,0,1:T(8,128)(2,1)S(1)}, bf16[2,1,112,1536]{3,2,0,1:T(8,128)(2,1)S(1)}, u32[]{:S(2)}, u32[]{:S(2)}) collective-permute-start(bf16[2,1,112,1536]{3,2,0,1:T(8,128)(2,1)S(1)} %maximum_bitcast_fusion), channel_id=1, source_target_pairs={{0,1},{1,2},{2,3},{3,4},{4,5},{5,6},{6,7},{7,8},{8,9},{9,10},{10,1... | collective-permute-start | bytes 2064392 | tf_op jit(solution)/shard_map/ppermute | solution.py:21
  295.9 180.7 %collective-permute-start.1 = (bf16[2,1,112,1536]{3,2,0,1:T(8,128)(2,1)S(1)}, bf16[2,1,112,1536]{3,2,0,1:T(8,128)(2,1)S(1)}, u32[]{:S(2)}, u32[]{:S(2)}) collective-permute-start(bf16[2,1,112,1536]{3,2,0,1:T(8,128)(2,1)S(1)} %maximum_bitcast_fusion), channel_id=1, source_target_pairs={{1,0},{2,1},{3,2},{4,3},{5,4},{6,5},{7,6},{8,7},{9,8},{10,9},{11,1... | collective-permute-start | bytes 2064392 | tf_op jit(solution)/shard_map/ppermute | solution.py:23
  478.6 1.6 copy-start.1
  485.3 7.1 %copy-start.3 = (bf16[112,1536]{1,0:T(8,128)(2,1)S(1)}, bf16[112,1536]{1,0:T(8,128)(2,1)}, u32[]{:S(2)}) copy-start(bf16[112,1536]{1,0:T(8,128)(2,1)} %param.11) | copy-start | bytes 1032196
  485.9 11.2 %collective-permute-start.2 = (bf16[112,1536]{0,1:T(8,128)(2,1)S(1)}, bf16[112,1536]{0,1:T(8,128)(2,1)S(1)}, u32[]{:S(2)}, u32[]{:S(2)}) collective-permute-start(bf16[112,1536]{0,1:T(8,128)(2,1)S(1)} %fusion.34), channel_id=1, source_target_pairs={{0,16},{16,32},{32,48},{48,64},{64,80},{80,96},{96,112},{112,128},... | collective-permute-start | bytes 1032200 | tf_op jit(solution)/shard_map/ppermute | solution.py:33
  497.6 19.5 %slice-start = ((s8[4718592]{0:T(1024)(128)(4,1)}), s8[4194304]{0:T(1024)(128)(4,1)S(1)}, s32[]{:S(2)}) async-start(s8[4718592]{0:T(1024)(128)(4,1)} %bitcast.54), calls=%async_computation.3 | async-start | bytes 8388608
  501.4 15.6 %slice-start.1 = ((s8[4718592]{0:T(1024)(128)(4,1)}), s8[524288]{0:T(1024)(128)(4,1)S(1)}, s32[]{:S(2)}) async-start(s8[4718592]{0:T(1024)(128)(4,1)} %bitcast.54), calls=%async_computation.4 | async-start | bytes 1048576
  505.3 44.6 %collective-permute-start.3 = (bf16[2,1,112,1536]{3,2,0,1:T(8,128)(2,1)S(1)}, bf16[2,1,112,1536]{3,2,0,1:T(8,128)(2,1)S(1)}, u32[]{:S(2)}, u32[]{:S(2)}) collective-permute-start(bf16[2,1,112,1536]{3,2,0,1:T(8,128)(2,1)S(1)} %maximum_bitcast_fusion.1), channel_id=1, source_target_pairs={{0,1},{1,2},{2,3},{3,4},{4,5},{5,6},{6,7},{7,8},{8,9},{9,10},{10,1... | collective-permute-start | bytes 2064392 | tf_op jit(solution)/shard_map/ppermute | solution.py:21
  507.2 66.2 %collective-permute-start.4 = (bf16[2,1,112,1536]{3,2,0,1:T(8,128)(2,1)S(1)}, bf16[2,1,112,1536]{3,2,0,1:T(8,128)(2,1)S(1)}, u32[]{:S(2)}, u32[]{:S(2)}) collective-permute-start(bf16[2,1,112,1536]{3,2,0,1:T(8,128)(2,1)S(1)} %maximum_bitcast_fusion.1), channel_id=1, source_target_pairs={{1,0},{2,1},{3,2},{4,3},{5,4},{6,5},{7,6},{8,7},{9,8},{10,9},{11,1... | collective-permute-start | bytes 2064392 | tf_op jit(solution)/shard_map/ppermute | solution.py:23
  575.4 1.6 copy-start
Sparse Core Ops, SparseCore 0:
  10.5 142.3 all-gather.3
  156.1 133.9 all-gather.5
  293.3 179.1 all-gather.7
where the time goes:
time: 598 us; the launch traced here: 590 us
  waiting for transfers between devices  499 us (83%)
  matrix products  30 us (5%)
  starting transfers between devices  29.9 us (5%)
  between operations  13.5 us (2%)
  local copies, waits for them, and re-layouts  12.7 us (2%)
    all_gather x1, waiting for transfers between devices, shards(): lax.all_gather(w_query, 'dp', axis=0, tiled=True)  167 us
    all_gather x1, waiting for transfers between devices, shards(): lax.all_gather(w_key, 'dp', axis=0, tiled=True)  137 us
    all_gather x1, waiting for transfers between devices, shards(): lax.all_gather(w_value, 'dp', axis=0, tiled=True)  133 us
    ppermute x2, waiting for transfers between devices, extended(): lax.ppermute(tail, axis, [(i, (i + 1) % count) for i in range(ends)])  31.1 us
    ppermute x2, waiting for transfers between devices, extended(): lax.ppermute(head, axis, [((i + 1) % count, i) for i in range(ends)])  23.6 us
    ppermute x2, starting transfers between devices, extended(): lax.ppermute(head, axis, [((i + 1) % count, i) for i in range(ends)])  19.5 us
  transfers between devices with their start and end apart: 8, of which 6 were waited for; matrix products, arithmetic and copies ran while one was open for 3% of the time, Pallas kernels for 0%

commit v1 on v0

v1 whole, which is shorter than its diff:
```python
import functools

import jax
import jax.numpy as jnp
from jax import lax
from jax.experimental import pallas as pl
from jax.experimental.pallas import tpu as pltpu
from jax.sharding import Mesh, PartitionSpec as P

HEADS = 12
HEAD_DIM = 128
D = HEADS * HEAD_DIM
BAND = 112
PER_SECTION = 16
SECTIONS = 32
DEVICES = SECTIONS * PER_SECTION
ROWS = D // PER_SECTION
HALF = 3 * D // 2
TILE = 256
FLAGS = 16
EPSILON = 1e-06
SHAPE = (4, 4, 2, 8, 2)
AXES = ("zl", "x", "core", "y", "zh")


def layer_norm(values):
    average = jnp.mean(values, axis=-1, keepdims=True)
    centred = values - average
    spread = jnp.mean(centred * centred, axis=-1, keepdims=True)
    return centred * lax.rsqrt(spread + EPSILON)


def attend(query, key, value, query_rows, first, bias):
    scores = lax.dot_general(
        query[query_rows : query_rows + BAND],
        key[first : first + 3 * BAND],
        (((1,), (1,)), ((), ())),
        preferred_element_type=jnp.float32,
    )
    scores = scores + bias
    peak = jnp.max(scores, axis=-1, keepdims=True)
    weights = jnp.exp2((scores - peak) * (HEAD_DIM**-0.5 * 1.4426950408889634))
    total = jnp.sum(weights, axis=-1, keepdims=True)
    mixed = jnp.dot(
        weights.astype(jnp.bfloat16),
        value[first : first + 3 * BAND],
        preferred_element_type=jnp.float32,
    )
    return (mixed / total).astype(jnp.bfloat16)


def compute(
    place,
    normed_ref,
    window_ref,
    bias_first_ref,
    gate_first_ref,
    mod_ref,
    bias_second_ref,
    gain_query_ref,
    gain_key_ref,
    own_ref,
    own_across_ref,
    far_ref,
    far_across_ref,
    out_ref,
    weights,
    query,
    key,
    value,
    advanced,
    normed,
    sem,
):
    frame, core, zh = place[0], place[1], place[2]
    copies = []
    for part, ref in enumerate((own_ref, far_ref, own_across_ref, far_across_ref)):
        half = core if part < 2 else 1 - core
        side = zh if part % 2 == 0 else 1 - zh
        columns = pl.ds(pl.multiple_of(half * HALF, 128), HALF)
        for y in range(8):
            rows = pl.ds(pl.multiple_of((2 * y + side) * ROWS, 32), ROWS)
            copies.append(
                pltpu.make_async_copy(
                    ref.at[pl.ds(y * ROWS, ROWS), :],
                    weights.at[rows, columns],
                    sem.at[part * 8 + y],
                )
            )
    for copy in copies:
        copy.start()
    for copy in copies:
        copy.wait()

    def project(source, bands):
        rows = bands * BAND
        inner = (bands - 2) * BAND

        def tile(index, rows_of):
            columns = pl.ds(pl.multiple_of(index * TILE, TILE), TILE)
            return jnp.dot(
                source[rows_of, :], weights[:, columns], preferred_element_type=jnp.float32
            )

        def folded(product):
            squares = product * product
            return squares[:, :128] + squares[:, 128:]

        def query_tile(i, power):
            product = tile(i, pl.ds(BAND, inner))
            query[:inner, pl.ds(pl.multiple_of(i * TILE, TILE), TILE)] = product
            return power + folded(product)

        def key_tile(i, power):
            product = tile(i + D // TILE, pl.ds(0, rows))
            key[:rows, pl.ds(pl.multiple_of(i * TILE, TILE), TILE)] = product
            return power + folded(product)

        def value_tile(i, carry):
            product = tile(i + 2 * (D // TILE), pl.ds(0, rows))
            value[:rows, pl.ds(pl.multiple_of(i * TILE, TILE), TILE)] = product.astype(jnp.bfloat16)
            return carry

        tiles = D // TILE
        query_power = lax.fori_loop(0, tiles, query_tile, jnp.zeros((inner, 128), jnp.float32))
        key_power = lax.fori_loop(0, tiles, key_tile, jnp.zeros((rows, 128), jnp.float32))
        lax.fori_loop(0, tiles, value_tile, 0)
        norm = lambda power: lax.rsqrt(jnp.sum(power, axis=-1, keepdims=True) * (1.0 / D) + EPSILON)
        return norm(query_power), norm(key_power)

    def heads_of(bands, query_norm, key_norm, biases, finish):
        rows = bands * BAND
        inner = (bands - 2) * BAND

        def one_head(h, carry):
            lanes = pl.ds(pl.multiple_of(h * HEAD_DIM, HEAD_DIM), HEAD_DIM)
            head_query = (query[:inner, lanes] * query_norm * gain_query_ref[:, lanes]).astype(jnp.bfloat16)
            head_key = (key[:rows, lanes] * key_norm * gain_key_ref[:, lanes]).astype(jnp.bfloat16)
            head_value = value[:rows, lanes]
            for band in range(bands - 2):
                attended = attend(head_query, head_key, head_value, band * BAND, band * BAND, biases[band])
                finish(band, lanes, attended.astype(jnp.float32))
            return carry

        lax.fori_loop(0, HEADS, one_head, 0)

    query_norm, key_norm = project(normed_ref, 5)

    def finish_first(band, lanes, attended):
        rows = slice(band * BAND, (band + 1) * BAND)
        held = window_ref[rows, lanes].astype(jnp.float32)
        moved = (held + gate_first_ref[band : band + 1, lanes] * attended).astype(jnp.bfloat16)
        advanced[rows, lanes] = jnp.where(frame + band - 1 < PER_SECTION, window_ref[rows, lanes], moved)

    heads_of(5, query_norm, key_norm, [bias_first_ref[b : b + 1, :] for b in range(3)], finish_first)

    for band in range(3):
        rows = slice(band * BAND, (band + 1) * BAND)
        level = layer_norm(advanced[rows, :].astype(jnp.float32))
        normed[rows, :] = (
            level * (1.0 + mod_ref[3 * band + 1 : 3 * band + 2, :]) + mod_ref[3 * band : 3 * band + 1, :]
        ).astype(jnp.bfloat16)

    query_norm, key_norm = project(normed, 3)

    def finish_second(band, lanes, attended):
        held = advanced[BAND : 2 * BAND, lanes].astype(jnp.float32)
        out_ref[:, lanes] = (held + mod_ref[5:6, lanes] * attended).astype(jnp.bfloat16)

    heads_of(3, query_norm, key_norm, [bias_second_ref[0:1, :]], finish_second)


def bias_of(flags):
    lane = jnp.arange(3 * BAND, dtype=jnp.int32) // BAND
    closed = jnp.where(lane == 0, flags[:, 0:1], jnp.where(lane == 2, flags[:, 1:2], 0.0))
    return closed * -1e30


def shards(
    stream, incoming, levels, bounds, mod_table, w_query, w_key, w_value, gain_query, gain_key
):
    core = lax.axis_index("core")
    zh = lax.axis_index("zh")
    frame = lax.axis_index(AXES)

    packed = jnp.concatenate([w_query, w_key, w_value], axis=1)
    half = jnp.where(core == 0, packed[:, :HALF], packed[:, HALF:])
    across = lambda block: lax.ppermute(block, "core", [(0, 1), (1, 0)])
    opposite = lax.ppermute(half, "zh", [(0, 1), (1, 0)])
    own = lax.all_gather(half, "y", axis=0, tiled=True)
    far = lax.all_gather(opposite, "y", axis=0, tiled=True)
    own_across = across(own)
    far_across = across(far)

    flag_pair = jnp.stack([bounds[0, 0] >= frame, bounds[0, 1] <= frame + 1]).astype(jnp.bfloat16)
    flag_rows = jnp.zeros((FLAGS, D), jnp.bfloat16).at[:2, :].set(flag_pair[:, None])
    bands, flags = [], []
    for k in range(-2, 3):
        block = stream
        if abs(k) < 2:
            wraps = frame + PER_SECTION - k >= DEVICES
            block = jnp.concatenate([jnp.where(wraps, incoming, stream), flag_rows], axis=0)
        route = [(d, (d + PER_SECTION - k) % DEVICES) for d in range(DEVICES)]
        got = lax.ppermute(block, AXES, route)
        bands.append(got[:BAND])
        if abs(k) < 2:
            flags.append(got[BAND : BAND + 2, 0].astype(jnp.float32))
    bias_first = bias_of(jnp.stack(flags))
    bias_second = bias_of(flag_pair.astype(jnp.float32)[None, :])

    def rows_at(step, band):
        section = jnp.clip(band // PER_SECTION, 0, SECTIONS - 1)
        return lax.dynamic_index_in_dim(mod_table, levels[step, section], 0, keepdims=False)

    first = [rows_at(0, frame - PER_SECTION + k) for k in range(-2, 3)]
    second = [rows_at(1, frame + k) for k in range(-1, 2)]
    normed = jnp.concatenate(
        [
            (layer_norm(band.astype(jnp.float32)) * (1.0 + row[1][None, :]) + row[0][None, :]).astype(
                jnp.bfloat16
            )
            for band, row in zip(bands, first)
        ],
        axis=0,
    )
    window = jnp.concatenate(bands[1:4], axis=0)
    gate_first = jnp.stack([row[2] for row in first[1:4]])
    mod_second = jnp.concatenate(second, axis=0)
    place = jnp.stack([frame, core, zh]).astype(jnp.int32)

    vmem = pl.BlockSpec(memory_space=pltpu.VMEM)
    anywhere = pl.BlockSpec(memory_space=pl.ANY)
    return pl.pallas_call(
        compute,
        out_shape=jax.ShapeDtypeStruct((BAND, D), jnp.bfloat16),
        in_specs=[pl.BlockSpec(memory_space=pltpu.SMEM)] + [vmem] * 8 + [anywhere] * 4,
        out_specs=vmem,
        scratch_shapes=[
            pltpu.VMEM((D, 3 * D), jnp.bfloat16),
            pltpu.VMEM((3 * BAND, D), jnp.float32),
            pltpu.VMEM((5 * BAND, D), jnp.float32),
            pltpu.VMEM((5 * BAND, D), jnp.bfloat16),
            pltpu.VMEM((3 * BAND, D), jnp.bfloat16),
            pltpu.VMEM((3 * BAND, D), jnp.bfloat16),
            pltpu.SemaphoreType.DMA((32,)),
        ],
        compiler_params=pltpu.CompilerParams(vmem_limit_bytes=48 * 1024 * 1024),
        cost_estimate=pl.CostEstimate(
            flops=12_000_000_000, bytes_accessed=20_000_000, transcendentals=2_000_000
        ),
        name="two_steps",
    )(
        place,
        normed,
        window,
        bias_first,
        gate_first,
        mod_second,
        bias_second,
        gain_query[None, :],
        gain_key[None, :],
        own,
        own_across,
        far,
        far_across,
    )


def solution(mesh):
    inner = Mesh(mesh.devices.reshape(SHAPE), AXES)
    queue_dp = P(AXES, None)
    dp = P(("y", "zh"), None)
    in_specs = (queue_dp, dp, P(), queue_dp, P(), dp, dp, dp, P(), P())
    return jax.shard_map(shards, mesh=inner, in_specs=in_specs, out_specs=queue_dp, check_vma=False)
```

time: 598 us -> 190 us (0.32); the launches traced: 590 us -> 189 us
  waiting for transfers between devices: 499 us -> 35.8 us
  Pallas kernels: 0 us -> 41 us
  starting transfers between devices: 29.9 us -> 62.1 us
  matrix products: 30 us -> 0 us
  between operations: 13.5 us -> 30.2 us
  other arithmetic: 5.39 us -> 12.7 us
    all_gather x3 -> x2, waiting for transfers between devices: 437 us -> 29.5 us  [the longest x1 29.5 us: shards(): far = lax.all_gather(opposite, 'y', axis=0, tiled=True)]
    ppermute x5 -> x8, waiting for transfers between devices: 59 us -> 6.31 us  [the longest x5 3.95 us: shards(): got = lax.ppermute(block, AXES, route)]
    pallas_call x0 -> x1, Pallas kernels: none -> 41 us  [shards(): pl.pallas_call(compute, out_shape=jax.ShapeDtypeStruct((BAND, D), jnp.bfl...]
    ppermute x5 -> x8, starting transfers between devices: 29.8 us -> 62.1 us  [the longest x5 34.3 us: shards(): got = lax.ppermute(block, AXES, route)]
    dot_general x8 -> x0, matrix products: 25.2 us -> none  [the longest x2 7.54 us: project(): jnp.dot(normed, full_key, preferred_element_type=jnp.float32)]
    another operation x4 -> x0, local copies, waits for them, and re-layouts: 6.38 us -> none  [the longest x2 3.2 us: finish(): key_block = beside_all[0].reshape(3 * tok_rows, HEADS, HEAD_DIM)]
  transfers between devices with their start and end apart: 8 -> 10, of which waited for: 6 -> 3; matrix products, arithmetic and copies ran while one was open for 3% -> 8% of each run, Pallas kernels for 0% -> 0%
where the time goes in v1:
time: 190 us; the launch traced here: 189 us
  starting transfers between devices  62.1 us (33%)
  Pallas kernels  41 us (22%)
  waiting for transfers between devices  35.8 us (19%)
  between operations  30.2 us (16%)
  other arithmetic  12.7 us (7%)
  local copies, waits for them, and re-layouts  6.98 us (4%)
    pallas_call x1, Pallas kernels, shards(): pl.pallas_call(compute, out_shape=jax.ShapeDtypeStruct((BAND, D), jnp.bfl...  41 us
    ppermute x5, starting transfers between devices, shards(): got = lax.ppermute(block, AXES, route)  34.3 us
    all_gather x1, waiting for transfers between devices, shards(): far = lax.all_gather(opposite, 'y', axis=0, tiled=True)  29.5 us
    ppermute x2, starting transfers between devices, shards(): across = lambda block: lax.ppermute(block, 'core', [(0, 1), (1, 0)])  16.4 us
    ppermute x1, starting transfers between devices, shards(): opposite = lax.ppermute(half, 'zh', [(0, 1), (1, 0)])  11.5 us
    ppermute x5, waiting for transfers between devices, shards(): got = lax.ppermute(block, AXES, route)  3.95 us
  transfers between devices with their start and end apart: 10, of which 3 were waited for; matrix products, arithmetic and copies ran while one was open for 8% of the time, Pallas kernels for 0%

profile of v1, /device:TPU:1, one launch (start us, length us, event | category | flops | bytes accessed | tf_op | source)
XLA Modules:
  0.0 188.8 jit_solution(721640885553331674)
XLA Ops:
  6.5 2.1 %fusion.30 = bf16[96,2304]{1,0:T(8,128)(2,1)} fusion(bf16[96,1536]{1,0:T(8,128)(2,1)} %param.19, bf16[96,1536]{1,0:T(8,128)(2,1)} %param.18, bf16[96,1536]{1,0:T(8,128)(2,1)} %param.17, pred[]{:T(512)S(6)} %eq.33), kind=kLoop, calls=%fused_computation.42 | loop fusion | flops 1990656 | bytes 1327105 | tf_op jit(solution)/shard_map/jit(_where)/select_n | solution.py:187
  8.7 11.5 %collective-permute-start.6 = (bf16[96,2304]{1,0:T(8,128)(2,1)}, bf16[96,2304]{1,0:T(8,128)(2,1)S(1)}, u32[]{:S(2)}, u32[]{:S(2)}) collective-permute-start(bf16[96,2304]{1,0:T(8,128)(2,1)} %fusion.30), channel_id=1, source_target_pairs={{0,1},{1,0},{2,3},{3,2},{4,5},{5,4},{6,7},{7,6},{8,9},{9,8},{10,11... | collective-permute-start | bytes 1327112 | tf_op jit(solution)/shard_map/ppermute | solution.py:189
  20.2 5.0 %collective-permute-start = (bf16[112,1536]{1,0:T(8,128)(2,1)S(1)}, bf16[112,1536]{1,0:T(8,128)(2,1)S(1)}, u32[]{:S(2)}, u32[]{:S(2)}) collective-permute-start(bf16[112,1536]{1,0:T(8,128)(2,1)S(1)} %copy-done.2), channel_id=1, source_target_pairs={{0,18},{1,19},{2,20},{3,21},{4,22},{5,23},{6,24},{7,25},{8,26},{9,... | collective-permute-start | bytes 1032200 | tf_op jit(solution)/shard_map/ppermute | solution.py:204
  25.2 2.4 %collective-permute-start.4 = (bf16[112,1536]{1,0:T(8,128)(2,1)S(1)}, bf16[112,1536]{1,0:T(8,128)(2,1)S(1)}, u32[]{:S(2)}, u32[]{:S(2)}) collective-permute-start(bf16[112,1536]{1,0:T(8,128)(2,1)S(1)} %copy-done.2), channel_id=1, source_target_pairs={{0,14},{1,15},{2,16},{3,17},{4,18},{5,19},{6,20},{7,21},{8,22},{9,... | collective-permute-start | bytes 1032200 | tf_op jit(solution)/shard_map/ppermute | solution.py:204
  29.6 0.8 copy-done
  30.6 1.2 pad_maximum_fusion.5
  31.8 10.8 %collective-permute-start.3 = (bf16[128,1536]{1,0:T(8,128)(2,1)}, bf16[128,1536]{1,0:T(8,128)(2,1)S(1)}, u32[]{:S(2)}, u32[]{:S(2)}) collective-permute-start(bf16[128,1536]{1,0:T(8,128)(2,1)} %get-tuple-element.54), channel_id=1, source_target_pairs={{0,15},{1,16},{2,17},{3,18},{4,19},{5,20},{6,21},{7,22},{8,23},{9,... | collective-permute-start | bytes 1179656 | tf_op jit(solution)/shard_map/ppermute | solution.py:204
  42.6 14.1 %collective-permute-start.2 = (bf16[128,1536]{1,0:T(8,128)(2,1)}, bf16[128,1536]{1,0:T(8,128)(2,1)S(1)}, u32[]{:S(2)}, u32[]{:S(2)}) collective-permute-start(bf16[128,1536]{1,0:T(8,128)(2,1)} %get-tuple-element.55), channel_id=1, source_target_pairs={{0,16},{1,17},{2,18},{3,19},{4,20},{5,21},{6,22},{7,23},{8,24},{9,... | collective-permute-start | bytes 1179656 | tf_op jit(solution)/shard_map/ppermute | solution.py:204
  56.7 1.9 %collective-permute-start.1 = (bf16[128,1536]{1,0:T(8,128)(2,1)}, bf16[128,1536]{1,0:T(8,128)(2,1)}, u32[]{:S(2)}, u32[]{:S(2)}) collective-permute-start(bf16[128,1536]{1,0:T(8,128)(2,1)} %get-tuple-element.56), channel_id=1, source_target_pairs={{0,17},{1,18},{2,19},{3,20},{4,21},{5,22},{6,23},{7,24},{8,25},{9,... | collective-permute-start | bytes 1179656 | tf_op jit(solution)/shard_map/ppermute | solution.py:204
  58.8 0.7 constant_dynamic-slice_fusion.10
  71.5 1.1 constant_dynamic-slice_fusion.2
  76.6 1.4 fusion.36
  78.0 1.2 fusion.44.bias_second_ref
  80.5 3.9 %collective-permute-done.1 = bf16[128,1536]{1,0:T(8,128)(2,1)} collective-permute-done((bf16[128,1536]{1,0:T(8,128)(2,1)}, bf16[128,1536]{1,0:T(8,128)(2,1)}, u32[]{:S(2)}, u32[]{:S(2)}) %collective-permute-start.1) | collective-permute-done | bytes 393248 | tf_op jit(solution)/shard_map/ppermute | solution.py:204
  84.5 0.8 slice_reduce_fusion.4
  85.5 1.1 convert_reduce_fusion.3
  87.2 13.8 %collective-permute-start.5 = (bf16[768,2304]{1,0:T(8,128)(2,1)}, bf16[768,2304]{1,0:T(8,128)(2,1)}, u32[]{:S(2)}, u32[]{:S(2)}) collective-permute-start(bf16[768,2304]{1,0:T(8,128)(2,1)} %all-gather.3.cloned.1.call-done.own_ref), channel_id=1, source_target_pairs={{0,16},{16,0},{1,17},{17,1},{2,18},{18,2},{3,19},{19,3},{4,20},{20... | collective-permute-start | bytes 10616840 | tf_op jit(solution)/shard_map/ppermute | solution.py:188
  101.0 29.5 %all-gather.5.cloned.1.call-done.far_ref = bf16[768,2304]{1,0:T(8,128)(2,1)} async-done(((bf16[96,2304]{1,0:T(8,128)(2,1)}), bf16[768,2304]{1,0:T(8,128)(2,1)}) %all-gather.5.cloned.1.call-update) | async-done | bytes 3538960 | tf_op jit(solution)/shard_map/all_gather | solution.py:191
  130.4 2.6 %collective-permute-start.7 = (bf16[768,2304]{1,0:T(8,128)(2,1)}, bf16[768,2304]{1,0:T(8,128)(2,1)S(1)}, u32[]{:S(2)}, u32[]{:S(2)}) collective-permute-start(bf16[768,2304]{1,0:T(8,128)(2,1)} %all-gather.5.cloned.1.call-done.far_ref), channel_id=1, source_target_pairs={{0,16},{16,0},{1,17},{17,1},{2,18},{18,2},{3,19},{19,3},{4,20},{20... | collective-permute-start | bytes 10616840 | tf_op jit(solution)/shard_map/ppermute | solution.py:188
  133.2 1.2 fusion.22
  134.6 1.2 fusion.46
  136.7 2.4 %collective-permute-done.7.far_across_ref = bf16[768,2304]{1,0:T(8,128)(2,1)S(1)} collective-permute-done((bf16[768,2304]{1,0:T(8,128)(2,1)}, bf16[768,2304]{1,0:T(8,128)(2,1)S(1)}, u32[]{:S(2)}, u32[]{:S(2)}) %collective-permute-start.7) | collective-permute-done | bytes 3538976 | tf_op jit(solution)/shard_map/ppermute | solution.py:188
  139.1 1.9 copy-done.7
  141.0 41.0 %two_steps.1 = bf16[112,1536]{1,0:T(8,128)(2,1)} custom-call(s32[3]{0:T(128)S(1)} %pad_add_fusion.1.place, bf16[560,1536]{1,0:T(8,128)(2,1)S(1)} %fusion.35.normed_ref, bf16[336,1536]{1,0:T(8,128)(2,1)S(1)} %pad_maximum_fusion.window_ref, f32[3,336]{1,0:T(4,128)S(1)} %select_multiply_fusion.bias_first_ref, f32[3,1536]{1,0:T(4,128)S(1)} %pad_maximum_fusion.7.gate_first_ref, ...), custom_call_target="tpu_custom_call" | custom-call | flops 12000000000 | bytes 20000000 | tf_op jit(solution)/shard_map/two_steps/pallas_call | solution.py:233
  (68 shorter events, 4.9 us)
Async XLA Ops:
  6.5 13.7 %copy-start.2 = (bf16[112,1536]{1,0:T(8,128)(2,1)S(1)}, bf16[112,1536]{1,0:T(8,128)(2,1)}, u32[]{:S(2)}) copy-start(bf16[112,1536]{1,0:T(8,128)(2,1)} %param.12) | copy-start | bytes 1032196
  6.5 21.1 %copy-start.6 = (s32[1,2]{1,0:T(1,128)S(1)}, s32[1,2]{1,0:T(1,128)}, u32[]{:S(2)}) copy-start(s32[1,2]{1,0:T(1,128)} %param.15) | copy-start | bytes 28
  6.5 23.9 %copy-start.1 = (bf16[112,1536]{1,0:T(8,128)(2,1)S(1)}, bf16[112,1536]{1,0:T(8,128)(2,1)}, u32[]{:S(2)}) copy-start(bf16[112,1536]{1,0:T(8,128)(2,1)} %param.13) | copy-start | bytes 1032196
  6.5 80.6 %all-gather.3.cloned.1.call-start = ((), (), s32[]{:S(2)}) async-start(), calls=%async_computation | async-start | bytes 3981312 | tf_op jit(solution)/shard_map/all_gather | solution.py:190
  8.7 121.7 %all-gather.5.cloned.1.call-start = ((), (), s32[]{:S(2)}) async-start(), calls=%async_computation.1 | async-start | bytes 3981312 | tf_op jit(solution)/shard_map/all_gather | solution.py:191
  8.7 20.8 %collective-permute-start.6 = (bf16[96,2304]{1,0:T(8,128)(2,1)}, bf16[96,2304]{1,0:T(8,128)(2,1)S(1)}, u32[]{:S(2)}, u32[]{:S(2)}) collective-permute-start(bf16[96,2304]{1,0:T(8,128)(2,1)} %fusion.30), channel_id=1, source_target_pairs={{0,1},{1,0},{2,3},{3,2},{4,5},{5,4},{6,7},{7,6},{8,9},{9,8},{10,11... | collective-permute-start | bytes 1327112 | tf_op jit(solution)/shard_map/ppermute | solution.py:189
  20.2 59.0 %collective-permute-start = (bf16[112,1536]{1,0:T(8,128)(2,1)S(1)}, bf16[112,1536]{1,0:T(8,128)(2,1)S(1)}, u32[]{:S(2)}, u32[]{:S(2)}) collective-permute-start(bf16[112,1536]{1,0:T(8,128)(2,1)S(1)} %copy-done.2), channel_id=1, source_target_pairs={{0,18},{1,19},{2,20},{3,21},{4,22},{5,23},{6,24},{7,25},{8,26},{9,... | collective-permute-start | bytes 1032200 | tf_op jit(solution)/shard_map/ppermute | solution.py:204
  25.2 54.2 %collective-permute-start.4 = (bf16[112,1536]{1,0:T(8,128)(2,1)S(1)}, bf16[112,1536]{1,0:T(8,128)(2,1)S(1)}, u32[]{:S(2)}, u32[]{:S(2)}) collective-permute-start(bf16[112,1536]{1,0:T(8,128)(2,1)S(1)} %copy-done.2), channel_id=1, source_target_pairs={{0,14},{1,15},{2,16},{3,17},{4,18},{5,19},{6,20},{7,21},{8,22},{9,... | collective-permute-start | bytes 1032200 | tf_op jit(solution)/shard_map/ppermute | solution.py:204
  29.6 0.8 copy-start
  30.5 28.4 %copy-start.3 = (s32[2,32]{1,0:T(2,128)S(1)}, s32[2,32]{1,0:T(2,128)}, u32[]{:S(2)}) copy-start(s32[2,32]{1,0:T(2,128)} %param.14) | copy-start | bytes 772
  30.6 39.0 %copy-start.4 = (f32[1536]{0:T(1024)S(1)}, f32[1536]{0:T(1024)}, u32[]{:S(2)}) copy-start(f32[1536]{0:T(1024)} %param.20) | copy-start | bytes 18436
  30.6 39.1 %copy-start.5 = (f32[1536]{0:T(1024)S(1)}, f32[1536]{0:T(1024)}, u32[]{:S(2)}) copy-start(f32[1536]{0:T(1024)} %param.21) | copy-start | bytes 18436
  31.8 48.5 %collective-permute-start.3 = (bf16[128,1536]{1,0:T(8,128)(2,1)}, bf16[128,1536]{1,0:T(8,128)(2,1)S(1)}, u32[]{:S(2)}, u32[]{:S(2)}) collective-permute-start(bf16[128,1536]{1,0:T(8,128)(2,1)} %get-tuple-element.54), channel_id=1, source_target_pairs={{0,15},{1,16},{2,17},{3,18},{4,19},{5,20},{6,21},{7,22},{8,23},{9,... | collective-permute-start | bytes 1179656 | tf_op jit(solution)/shard_map/ppermute | solution.py:204
  42.6 37.8 %collective-permute-start.2 = (bf16[128,1536]{1,0:T(8,128)(2,1)}, bf16[128,1536]{1,0:T(8,128)(2,1)S(1)}, u32[]{:S(2)}, u32[]{:S(2)}) collective-permute-start(bf16[128,1536]{1,0:T(8,128)(2,1)} %get-tuple-element.55), channel_id=1, source_target_pairs={{0,16},{1,17},{2,18},{3,19},{4,20},{5,21},{6,22},{7,23},{8,24},{9,... | collective-permute-start | bytes 1179656 | tf_op jit(solution)/shard_map/ppermute | solution.py:204
  56.7 27.7 %collective-permute-start.1 = (bf16[128,1536]{1,0:T(8,128)(2,1)}, bf16[128,1536]{1,0:T(8,128)(2,1)}, u32[]{:S(2)}, u32[]{:S(2)}) collective-permute-start(bf16[128,1536]{1,0:T(8,128)(2,1)} %get-tuple-element.56), channel_id=1, source_target_pairs={{0,17},{1,18},{2,19},{3,20},{4,21},{5,22},{6,23},{7,24},{8,25},{9,... | collective-permute-start | bytes 1179656 | tf_op jit(solution)/shard_map/ppermute | solution.py:204
  87.2 49.5 %collective-permute-start.5 = (bf16[768,2304]{1,0:T(8,128)(2,1)}, bf16[768,2304]{1,0:T(8,128)(2,1)}, u32[]{:S(2)}, u32[]{:S(2)}) collective-permute-start(bf16[768,2304]{1,0:T(8,128)(2,1)} %all-gather.3.cloned.1.call-done.own_ref), channel_id=1, source_target_pairs={{0,16},{16,0},{1,17},{17,1},{2,18},{18,2},{3,19},{19,3},{4,20},{20... | collective-permute-start | bytes 10616840 | tf_op jit(solution)/shard_map/ppermute | solution.py:188
  130.4 8.7 %collective-permute-start.7 = (bf16[768,2304]{1,0:T(8,128)(2,1)}, bf16[768,2304]{1,0:T(8,128)(2,1)S(1)}, u32[]{:S(2)}, u32[]{:S(2)}) collective-permute-start(bf16[768,2304]{1,0:T(8,128)(2,1)} %all-gather.5.cloned.1.call-done.far_ref), channel_id=1, source_target_pairs={{0,16},{16,0},{1,17},{17,1},{2,18},{18,2},{3,19},{19,3},{4,20},{20... | collective-permute-start | bytes 10616840 | tf_op jit(solution)/shard_map/ppermute | solution.py:188
  139.1 1.9 copy-start.7
Sparse Core Ops, SparseCore 0:
  9.4 69.3 all-gather.2
  80.9 49.4 all-gather.4

commit v2 on v1

v2 whole, which is shorter than its diff:
```python
import jax
import jax.numpy as jnp
from jax import lax
from jax.experimental import pallas as pl
from jax.experimental.pallas import tpu as pltpu
from jax.sharding import Mesh, PartitionSpec as P

HEADS = 12
HEAD_DIM = 128
D = HEADS * HEAD_DIM
BAND = 112
PER_SECTION = 16
SECTIONS = 32
DEVICES = SECTIONS * PER_SECTION
LEVELS = 32
ROWS = D // PER_SECTION
HALF = 3 * D // 2
TILE = 768
FLAGS = 16
EPSILON = 1e-06
SHAPE = (4, 4, 2, 8, 2)
AXES = ("zl", "x", "core", "y", "zh")
SCALE = HEAD_DIM**-0.5 * 1.4426950408889634


def layer_norm(values):
    average = jnp.mean(values, axis=-1, keepdims=True)
    centred = values - average
    spread = jnp.mean(centred * centred, axis=-1, keepdims=True)
    return centred * lax.rsqrt(spread + EPSILON)


def level_of(levels, step, band):
    section = lax.div(jnp.clip(band, 0, DEVICES - 1), jnp.int32(PER_SECTION))
    return levels[step, section]


def mod_row(mod_ref, part, level):
    return mod_ref[pl.ds(part * LEVELS + level, 1), :]


def modulated(values, mod_ref, level):
    normed = layer_norm(values.astype(jnp.float32))
    return (normed * (1.0 + mod_row(mod_ref, 1, level)) + mod_row(mod_ref, 0, level)).astype(jnp.bfloat16)


def prepare(place, levels, mod_ref, *rest):
    out_ref = rest[-1]
    for i in range(5):
        level = level_of(levels, 0, place[0] - PER_SECTION + i - 2)
        out_ref[i * BAND : (i + 1) * BAND, :] = modulated(rest[i][:BAND, :], mod_ref, level)


def attend(query, key, value, first, bias):
    scores = lax.dot_general(
        query[first : first + BAND],
        key[first : first + 3 * BAND],
        (((1,), (1,)), ((), ())),
        preferred_element_type=jnp.float32,
    )
    scores = scores + bias
    peak = jnp.max(scores, axis=-1, keepdims=True)
    weights = jnp.exp2(scores - peak).astype(jnp.bfloat16)
    mixed = jnp.dot(weights, value[first : first + 3 * BAND], preferred_element_type=jnp.float32)
    return (mixed[:, :HEAD_DIM] / mixed[:, HEAD_DIM:]).astype(jnp.bfloat16)


def bias_row(previous, following):
    lane = lax.broadcasted_iota(jnp.int32, (1, 3 * BAND), 1)
    closed = jnp.where(lane < BAND, previous, jnp.where(lane >= 2 * BAND, following, 0.0))
    return closed * -1e30


def compute(
    place,
    levels,
    bounds,
    mod_ref,
    normed_ref,
    before_ref,
    middle_ref,
    after_ref,
    gain_query_ref,
    gain_key_ref,
    gathered_ref,
    out_ref,
    weights,
    query,
    key,
    value,
    advanced,
    normed,
    gates,
    sem,
):
    frame = place[0]
    windows = (before_ref, middle_ref, after_ref)

    def copy_of(tile, y):
        core, first = divmod(tile * TILE, HALF)
        block = (2 * y + core) * 2 * ROWS
        return pltpu.make_async_copy(
            gathered_ref.at[pl.ds(block, 2 * ROWS), pl.ds(first, TILE)],
            weights.at[pl.ds(y * 2 * ROWS, 2 * ROWS), pl.ds(tile * TILE, TILE)],
            sem.at[tile * 8 + y],
        )

    for tile in range(6):
        for y in range(8):
            copy_of(tile, y).start()

    def arrived(tile):
        for y in range(8):
            copy_of(tile, y).wait()

    def project(source, bands, first_use):
        rows = bands * BAND
        inner = (bands - 2) * BAND

        def tile(index, rows_of):
            return jnp.dot(
                source[rows_of, :],
                weights[:, index * TILE : (index + 1) * TILE],
                preferred_element_type=jnp.float32,
            )

        def folded(product):
            squares = product * product
            return sum(squares[:, i : i + 128] for i in range(0, TILE, 128))

        def norm(power):
            return lax.rsqrt(jnp.sum(power, axis=-1, keepdims=True) * (1.0 / D) + EPSILON)

        query_power = key_power = 0.0
        for i in range(2):
            if first_use:
                arrived(i)
            product = tile(i, slice(BAND, BAND + inner))
            query[:inner, i * TILE : (i + 1) * TILE] = product
            query_power = query_power + folded(product)
        for i in range(2):
            if first_use:
                arrived(2 + i)
            product = tile(2 + i, slice(0, rows))
            key[:rows, i * TILE : (i + 1) * TILE] = product
            key_power = key_power + folded(product)
        for i in range(2):
            if first_use:
                arrived(4 + i)
            value[:rows, i * TILE : (i + 1) * TILE] = tile(4 + i, slice(0, rows)).astype(jnp.bfloat16)
        return norm(query_power), norm(key_power)

    def heads_of(bands, query_norm, key_norm, biases, finish):
        rows = bands * BAND
        inner = (bands - 2) * BAND

        def one_head(h, carry):
            lanes = pl.ds(pl.multiple_of(h * HEAD_DIM, HEAD_DIM), HEAD_DIM)
            head_query = (query[:inner, lanes] * query_norm * (gain_query_ref[:, lanes] * SCALE)).astype(jnp.bfloat16)
            head_key = (key[:rows, lanes] * key_norm * gain_key_ref[:, lanes]).astype(jnp.bfloat16)
            head_value = jnp.concatenate(
                [value[:rows, lanes], jnp.ones((rows, HEAD_DIM), jnp.bfloat16)], axis=1
            )
            for band in range(bands - 2):
                attended = attend(head_query, head_key, head_value, band * BAND, biases[band])
                finish(band, lanes, attended.astype(jnp.float32))
            return carry

        lax.fori_loop(0, HEADS, one_head, 0, unroll=4)

    query_norm, key_norm = project(normed_ref, 5, True)

    biases = []
    for window in windows:
        flags = window[BAND : BAND + FLAGS, : 3 * BAND].astype(jnp.float32)
        biases.append(bias_row(flags[0:1], flags[1:2]))

    for band in range(3):
        gates[band : band + 1, :] = mod_row(mod_ref, 2, level_of(levels, 0, frame - PER_SECTION + band - 1))
    gates[3:4, :] = mod_row(mod_ref, 2, level_of(levels, 1, frame))

    def finish_first(band, lanes, attended):
        gate = gates[band : band + 1, lanes]
        held = windows[band][:BAND, lanes]
        moved = (held.astype(jnp.float32) + gate * attended).astype(jnp.bfloat16)
        entering = jnp.where(frame + band - 1 < PER_SECTION, held, moved)
        advanced[band * BAND : (band + 1) * BAND, lanes] = entering

    heads_of(5, query_norm, key_norm, biases, finish_first)

    for band in range(3):
        rows = slice(band * BAND, (band + 1) * BAND)
        normed[rows, :] = modulated(advanced[rows, :], mod_ref, level_of(levels, 1, frame + band - 1))

    query_norm, key_norm = project(normed, 3, False)

    bias_second = bias_row(
        jnp.where(bounds[0, 0] >= frame, 1.0, 0.0), jnp.where(bounds[0, 1] <= frame + 1, 1.0, 0.0)
    )

    def finish_second(band, lanes, attended):
        gate = gates[3:4, lanes]
        held = advanced[BAND : 2 * BAND, lanes].astype(jnp.float32)
        out_ref[:, lanes] = (held + gate * attended).astype(jnp.bfloat16)

    heads_of(3, query_norm, key_norm, [bias_second], finish_second)


def prepared(place, levels, table, bands):
    smem = pl.BlockSpec(memory_space=pltpu.SMEM)
    vmem = pl.BlockSpec(memory_space=pltpu.VMEM)
    return pl.pallas_call(
        prepare,
        out_shape=jax.ShapeDtypeStruct((5 * BAND, D), jnp.bfloat16),
        in_specs=[smem] * 2 + [vmem] * 6,
        out_specs=vmem,
        compiler_params=pltpu.CompilerParams(vmem_limit_bytes=16 * 1024 * 1024),
        cost_estimate=pl.CostEstimate(flops=10_000_000, bytes_accessed=4_000_000, transcendentals=0),
        name="normed_window",
    )(place, levels, table, *bands)


def two_steps(place, levels, bounds, table, normed, windows, gain_query, gain_key, gathered):
    smem = pl.BlockSpec(memory_space=pltpu.SMEM)
    vmem = pl.BlockSpec(memory_space=pltpu.VMEM)
    anywhere = pl.BlockSpec(memory_space=pl.ANY)
    return pl.pallas_call(
        compute,
        out_shape=jax.ShapeDtypeStruct((BAND, D), jnp.bfloat16),
        in_specs=[smem] * 3 + [vmem] * 7 + [anywhere],
        out_specs=vmem,
        scratch_shapes=[
            pltpu.VMEM((D, 3 * D), jnp.bfloat16),
            pltpu.VMEM((3 * BAND, D), jnp.float32),
            pltpu.VMEM((5 * BAND, D), jnp.float32),
            pltpu.VMEM((5 * BAND, D), jnp.bfloat16),
            pltpu.VMEM((3 * BAND, D), jnp.bfloat16),
            pltpu.VMEM((3 * BAND, D), jnp.bfloat16),
            pltpu.VMEM((8, D), jnp.float32),
            pltpu.SemaphoreType.DMA((48,)),
        ],
        compiler_params=pltpu.CompilerParams(vmem_limit_bytes=48 * 1024 * 1024),
        cost_estimate=pl.CostEstimate(
            flops=12_000_000_000, bytes_accessed=20_000_000, transcendentals=2_000_000
        ),
        name="two_steps",
    )(place, levels, bounds, table, normed, *windows, gain_query, gain_key, gathered)


def tied(value, *others):
    return lax.optimization_barrier((value, *others))[0]


def shards(
    stream, incoming, levels, bounds, mod_table, w_query, w_key, w_value, gain_query, gain_key
):
    core = lax.axis_index("core")
    frame = lax.axis_index(AXES)
    zh = lax.axis_index("zh")
    place = frame.astype(jnp.int32)[None]

    half = jnp.where(
        core == 0,
        jnp.concatenate([w_query, w_key[:, : HALF - D]], axis=1),
        jnp.concatenate([w_key[:, HALF - D :], w_value], axis=1),
    )
    opposite = lax.ppermute(half, "zh", [(0, 1), (1, 0)])
    both = jnp.where(
        zh == 0, jnp.concatenate([half, opposite], axis=0), jnp.concatenate([opposite, half], axis=0)
    )
    gathered = lax.all_gather(both, ("y", "core"), axis=0, tiled=True)

    row = lax.broadcasted_iota(jnp.int32, (FLAGS, D), 0)
    flags = jnp.where(row == 0, bounds[0, 0] >= frame, bounds[0, 1] <= frame + 1).astype(jnp.bfloat16)
    last = frame >= DEVICES - PER_SECTION
    payloads = {
        -2: stream,
        -1: jnp.concatenate([jnp.where(last, incoming, stream), flags], axis=0),
        1: jnp.concatenate([jnp.where(frame > DEVICES - PER_SECTION, incoming, stream), flags], axis=0),
        2: stream,
    }
    payloads[0] = payloads[-1]
    bands = {}
    for k in range(-2, 3):
        route = [(d, (d + PER_SECTION - k) % DEVICES) for d in range(DEVICES)]
        bands[k] = lax.ppermute(tied(payloads[k], opposite), AXES, route)

    table = mod_table.transpose(1, 0, 2).reshape(3 * LEVELS, D)
    normed = prepared(place, levels, table, [bands[k] for k in range(-2, 3)])
    return two_steps(
        place,
        levels,
        bounds,
        table,
        normed,
        [bands[k] for k in (-1, 0, 1)],
        gain_query[None, :],
        gain_key[None, :],
        gathered,
    )


def solution(mesh):
    inner = Mesh(mesh.devices.reshape(SHAPE), AXES)
    queue_dp = P(AXES, None)
    dp = P(("y", "zh"), None)
    in_specs = (queue_dp, dp, P(), queue_dp, P(), dp, dp, dp, P(), P())
    return jax.shard_map(shards, mesh=inner, in_specs=in_specs, out_specs=queue_dp, check_vma=False)
```

time: 190 us -> 192 us (1.011)
  the two profiles are of different devices: /device:TPU:1 before, /device:TPU:199 now
where the time goes in v2:
time: 192 us
  waiting for transfers between devices  112 us (58%)
  starting transfers between devices  35.2 us (18%)
  Pallas kernels  25.3 us (13%)
  between operations  15 us (8%)
  other arithmetic  2.55 us (1%)
    all_gather x1, waiting for transfers between devices, shards(): gathered = lax.all_gather(both, ('y', 'core'), axis=0, tiled=True)  50.9 us
    ppermute x5, waiting for transfers between devices, shards(): bands[k] = lax.ppermute(tied(payloads[k], opposite), AXES, route)  47.4 us
    ppermute x5, starting transfers between devices, shards(): bands[k] = lax.ppermute(tied(payloads[k], opposite), AXES, route)  27.2 us
    pallas_call x1, Pallas kernels, two_steps(): pl.pallas_call(compute, out_shape=jax.ShapeDtypeStruct((BAND, D), jnp.bfl...  23.5 us
    ppermute x1, waiting for transfers between devices, shards(): opposite = lax.ppermute(half, 'zh', [(0, 1), (1, 0)])  13.9 us
    ppermute x1, starting transfers between devices, shards(): opposite = lax.ppermute(half, 'zh', [(0, 1), (1, 0)])  7.94 us
  transfers between devices with their start and end apart: 7, of which 3 were waited for; matrix products, arithmetic and copies ran while one was open for 1% of the time, Pallas kernels for 1%

profile of v2, /device:TPU:199, one launch (start us, length us, event | category | flops | bytes accessed | tf_op | source)
XLA Modules:
  0.0 191.9 jit_solution(18215954181087279936)
XLA Ops:
  6.5 1.0 fusion
  7.5 0.0 copy-start.1
  7.6 0.0 copy-start.3
  7.6 0.0 copy-start.4
  7.6 1.2 maximum_select_fusion.1
  8.8 7.9 %collective-permute-start = (bf16[96,2304]{1,0:T(8,128)(2,1)S(1)}, bf16[96,2304]{1,0:T(8,128)(2,1)S(1)}, u32[]{:S(2)}, u32[]{:S(2)}) collective-permute-start(bf16[96,2304]{1,0:T(8,128)(2,1)S(1)} %maximum_select_fusion.1), channel_id=1, source_target_pairs={{0,1},{1,0},{2,3},{3,2},{4,5},{5,4},{6,7},{7,6},{8,9},{9,8},{10,11... | collective-permute-start | bytes 1327112 | tf_op jit(solution)/shard_map/ppermute | solution.py:267
  16.8 13.9 %collective-permute-done = bf16[96,2304]{1,0:T(8,128)(2,1)S(1)} collective-permute-done((bf16[96,2304]{1,0:T(8,128)(2,1)S(1)}, bf16[96,2304]{1,0:T(8,128)(2,1)S(1)}, u32[]{:S(2)}, u32[]{:S(2)}) %collective-permute-start) | collective-permute-done | bytes 442400 | tf_op jit(solution)/shard_map/ppermute | solution.py:267
  30.6 1.1 maximum_select_fusion
  31.7 0.0 all-gather.2.cloned.1.call-update
  31.8 0.7 fusion.1
  33.8 0.1 pad.7.clone
  33.9 0.2 pad_maximum_fusion.1
  34.1 1.9 %collective-permute-start.3 = (bf16[128,1536]{1,0:T(8,128)(2,1)S(1)}, bf16[128,1536]{1,0:T(8,128)(2,1)S(1)}, u32[]{:S(2)}, u32[]{:S(2)}) collective-permute-start(bf16[128,1536]{1,0:T(8,128)(2,1)S(1)} %get-tuple-element.9), channel_id=1, source_target_pairs={{0,16},{1,17},{2,18},{3,19},{4,20},{5,21},{6,22},{7,23},{8,24},{9,... | collective-permute-start | bytes 1179656 | tf_op jit(solution)/shard_map/ppermute | solution.py:286
  36.1 11.0 %collective-permute-start.2 = (bf16[128,1536]{1,0:T(8,128)(2,1)S(1)}, bf16[128,1536]{1,0:T(8,128)(2,1)S(1)}, u32[]{:S(2)}, u32[]{:S(2)}) collective-permute-start(bf16[128,1536]{1,0:T(8,128)(2,1)S(1)} %get-tuple-element.9), channel_id=1, source_target_pairs={{0,17},{1,18},{2,19},{3,20},{4,21},{5,22},{6,23},{7,24},{8,25},{9,... | collective-permute-start | bytes 1179656 | tf_op jit(solution)/shard_map/ppermute | solution.py:286
  47.1 7.8 %collective-permute-start.4 = (bf16[128,1536]{1,0:T(8,128)(2,1)S(1)}, bf16[128,1536]{1,0:T(8,128)(2,1)S(1)}, u32[]{:S(2)}, u32[]{:S(2)}) collective-permute-start(bf16[128,1536]{1,0:T(8,128)(2,1)S(1)} %get-tuple-element.10), channel_id=1, source_target_pairs={{0,15},{1,16},{2,17},{3,18},{4,19},{5,20},{6,21},{7,22},{8,23},{9,... | collective-permute-start | bytes 1179656 | tf_op jit(solution)/shard_map/ppermute | solution.py:286
  54.9 1.9 %collective-permute-start.5 = (bf16[112,1536]{1,0:T(8,128)(2,1)S(1)}, bf16[112,1536]{1,0:T(8,128)(2,1)S(1)}, u32[]{:S(2)}, u32[]{:S(2)}) collective-permute-start(bf16[112,1536]{1,0:T(8,128)(2,1)S(1)} %copy-done.4), channel_id=1, source_target_pairs={{0,14},{1,15},{2,16},{3,17},{4,18},{5,19},{6,20},{7,21},{8,22},{9,... | collective-permute-start | bytes 1032200 | tf_op jit(solution)/shard_map/ppermute | solution.py:286
  56.8 4.6 %collective-permute-start.1 = (bf16[112,1536]{1,0:T(8,128)(2,1)S(1)}, bf16[112,1536]{1,0:T(8,128)(2,1)S(1)}, u32[]{:S(2)}, u32[]{:S(2)}) collective-permute-start(bf16[112,1536]{1,0:T(8,128)(2,1)S(1)} %copy-done.4), channel_id=1, source_target_pairs={{0,18},{1,19},{2,20},{3,21},{4,22},{5,23},{6,24},{7,25},{8,26},{9,... | collective-permute-start | bytes 1032200 | tf_op jit(solution)/shard_map/ppermute | solution.py:286
  61.5 47.4 %collective-permute-done.5.rest_4_ = bf16[112,1536]{1,0:T(8,128)(2,1)S(1)} collective-permute-done((bf16[112,1536]{1,0:T(8,128)(2,1)S(1)}, bf16[112,1536]{1,0:T(8,128)(2,1)S(1)}, u32[]{:S(2)}, u32[]{:S(2)}) %collective-permute-start.5) | collective-permute-done | bytes 344096 | tf_op jit(solution)/shard_map/ppermute | solution.py:286
  108.8 0.0 collective-permute-done.1.rest_0_
  108.8 0.0 collective-permute-done.3.rest_2_.middle_ref
  108.8 0.0 collective-permute-done.4.rest_3_.after_ref
  108.9 1.8 normed_window.1.normed_ref
  110.7 50.9 %all-gather.2.cloned.1.call-done.gathered_ref = bf16[3072,2304]{1,0:T(8,128)(2,1)} async-done(((bf16[192,2304]{1,0:T(8,128)(2,1)}), bf16[3072,2304]{1,0:T(8,128)(2,1)}) %all-gather.2.cloned.1.call-update) | async-done | bytes 14155792 | tf_op jit(solution)/shard_map/all_gather | solution.py:271
  161.6 23.5 %two_steps.1 = bf16[112,1536]{1,0:T(8,128)(2,1)} custom-call(s32[1]{0:T(128)} %bitcast.place, s32[2,32]{1,0:T(2,128)S(1)} %copy-done.2, s32[1,2]{1,0:T(1,128)S(1)} %copy-done.1, f32[96,1536]{1,0:T(8,128)S(1)} %bitcast.7, bf16[560,1536]{1,0:T(8,128)(2,1)S(1)} %normed_window.1.normed_ref, bf16[128,1536]{1,0:T(8,128)(2,1)S(1)} %collective-permute-done.2.rest_1_.before_ref, ...), custom_call_target="tpu_custom_call" | custom-call | flops 12000000000 | bytes 20000000 | tf_op jit(solution)/shard_map/two_steps/pallas_call | solution.py:227
  (17 shorter events, 0.1 us)
Async XLA Ops:
  6.5 155.0 %all-gather.2.cloned.1.call-start = ((), (), s32[]{:S(2)}) async-start(), calls=%async_computation | async-start | bytes 15040512 | tf_op jit(solution)/shard_map/all_gather | solution.py:271
  7.5 24.2 %copy-start.1 = (s32[1,2]{1,0:T(1,128)S(1)}, s32[1,2]{1,0:T(1,128)}, u32[]{:S(2)}) copy-start(s32[1,2]{1,0:T(1,128)} %bounds.1) | copy-start | bytes 28
  7.6 26.3 %copy-start.3 = (bf16[112,1536]{1,0:T(8,128)(2,1)S(1)}, bf16[112,1536]{1,0:T(8,128)(2,1)}, u32[]{:S(2)}) copy-start(bf16[112,1536]{1,0:T(8,128)(2,1)} %param.11) | copy-start | bytes 1032196
  7.6 26.3 %copy-start.4 = (bf16[112,1536]{1,0:T(8,128)(2,1)S(1)}, bf16[112,1536]{1,0:T(8,128)(2,1)}, u32[]{:S(2)}) copy-start(bf16[112,1536]{1,0:T(8,128)(2,1)} %param.10) | copy-start | bytes 1032196
  8.8 21.8 %collective-permute-start = (bf16[96,2304]{1,0:T(8,128)(2,1)S(1)}, bf16[96,2304]{1,0:T(8,128)(2,1)S(1)}, u32[]{:S(2)}, u32[]{:S(2)}) collective-permute-start(bf16[96,2304]{1,0:T(8,128)(2,1)S(1)} %maximum_select_fusion.1), channel_id=1, source_target_pairs={{0,1},{1,0},{2,3},{3,2},{4,5},{5,4},{6,7},{7,6},{8,9},{9,8},{10,11... | collective-permute-start | bytes 1327112 | tf_op jit(solution)/shard_map/ppermute | solution.py:267
  31.7 29.7 %copy-start.5 = (f32[1536]{0:T(1024)S(1)}, f32[1536]{0:T(1024)}, u32[]{:S(2)}) copy-start(f32[1536]{0:T(1024)} %param.18) | copy-start | bytes 18436
  31.7 29.7 %copy-start.6 = (f32[1536]{0:T(1024)S(1)}, f32[1536]{0:T(1024)}, u32[]{:S(2)}) copy-start(f32[1536]{0:T(1024)} %param.19) | copy-start | bytes 18436
  31.7 77.1 %copy-start = (f32[32,3,1536]{2,0,1:T(8,128)S(1)}, f32[32,3,1536]{2,0,1:T(8,128)}, u32[]{:S(2)}) copy-start(f32[32,3,1536]{2,0,1:T(8,128)} %param.14) | copy-start | bytes 1769476
  31.7 77.1 %copy-start.2 = (s32[2,32]{1,0:T(2,128)S(1)}, s32[2,32]{1,0:T(2,128)}, u32[]{:S(2)}) copy-start(s32[2,32]{1,0:T(2,128)} %levels.3) | copy-start | bytes 772
  34.1 74.7 %collective-permute-start.3 = (bf16[128,1536]{1,0:T(8,128)(2,1)S(1)}, bf16[128,1536]{1,0:T(8,128)(2,1)S(1)}, u32[]{:S(2)}, u32[]{:S(2)}) collective-permute-start(bf16[128,1536]{1,0:T(8,128)(2,1)S(1)} %get-tuple-element.9), channel_id=1, source_target_pairs={{0,16},{1,17},{2,18},{3,19},{4,20},{5,21},{6,22},{7,23},{8,24},{9,... | collective-permute-start | bytes 1179656 | tf_op jit(solution)/shard_map/ppermute | solution.py:286
  36.1 72.8 %collective-permute-start.2 = (bf16[128,1536]{1,0:T(8,128)(2,1)S(1)}, bf16[128,1536]{1,0:T(8,128)(2,1)S(1)}, u32[]{:S(2)}, u32[]{:S(2)}) collective-permute-start(bf16[128,1536]{1,0:T(8,128)(2,1)S(1)} %get-tuple-element.9), channel_id=1, source_target_pairs={{0,17},{1,18},{2,19},{3,20},{4,21},{5,22},{6,23},{7,24},{8,25},{9,... | collective-permute-start | bytes 1179656 | tf_op jit(solution)/shard_map/ppermute | solution.py:286
  47.1 61.7 %collective-permute-start.4 = (bf16[128,1536]{1,0:T(8,128)(2,1)S(1)}, bf16[128,1536]{1,0:T(8,128)(2,1)S(1)}, u32[]{:S(2)}, u32[]{:S(2)}) collective-permute-start(bf16[128,1536]{1,0:T(8,128)(2,1)S(1)} %get-tuple-element.10), channel_id=1, source_target_pairs={{0,15},{1,16},{2,17},{3,18},{4,19},{5,20},{6,21},{7,22},{8,23},{9,... | collective-permute-start | bytes 1179656 | tf_op jit(solution)/shard_map/ppermute | solution.py:286
  54.9 53.9 %collective-permute-start.5 = (bf16[112,1536]{1,0:T(8,128)(2,1)S(1)}, bf16[112,1536]{1,0:T(8,128)(2,1)S(1)}, u32[]{:S(2)}, u32[]{:S(2)}) collective-permute-start(bf16[112,1536]{1,0:T(8,128)(2,1)S(1)} %copy-done.4), channel_id=1, source_target_pairs={{0,14},{1,15},{2,16},{3,17},{4,18},{5,19},{6,20},{7,21},{8,22},{9,... | collective-permute-start | bytes 1032200 | tf_op jit(solution)/shard_map/ppermute | solution.py:286
  56.8 52.0 %collective-permute-start.1 = (bf16[112,1536]{1,0:T(8,128)(2,1)S(1)}, bf16[112,1536]{1,0:T(8,128)(2,1)S(1)}, u32[]{:S(2)}, u32[]{:S(2)}) collective-permute-start(bf16[112,1536]{1,0:T(8,128)(2,1)S(1)} %copy-done.4), channel_id=1, source_target_pairs={{0,18},{1,19},{2,20},{3,21},{4,22},{5,23},{6,24},{7,25},{8,26},{9,... | collective-permute-start | bytes 1032200 | tf_op jit(solution)/shard_map/ppermute | solution.py:286
Sparse Core Ops, SparseCore 0:
  31.9 129.6 all-gather.1

commit v3 on v2

v3 whole, which is shorter than its diff:
```python
import jax
import jax.numpy as jnp
from jax import lax
from jax.experimental import pallas as pl
from jax.experimental.pallas import tpu as pltpu
from jax.sharding import Mesh, PartitionSpec as P

HEADS = 12
HEAD_DIM = 128
D = HEADS * HEAD_DIM
BAND = 112
PER_SECTION = 16
SECTIONS = 32
DEVICES = SECTIONS * PER_SECTION
LEVELS = 32
ROWS = D // PER_SECTION
HALF = 3 * D // 2
COPY = 768
TILES = ((0, 768), (768, 1536), (1536, 2304), (2304, 3072), (3072, 4608))
FLAGS = 16
HELD = BAND + FLAGS
EPSILON = 1e-06
SHAPE = (4, 4, 2, 8, 2)
AXES = ("zl", "x", "core", "y", "zh")
SCALE = HEAD_DIM**-0.5 * 1.4426950408889634


def layer_norm(values):
    average = jnp.mean(values, axis=-1, keepdims=True)
    centred = values - average
    spread = jnp.mean(centred * centred, axis=-1, keepdims=True)
    return centred * lax.rsqrt(spread + EPSILON)


def level_of(levels, step, band):
    section = lax.div(jnp.clip(band, 0, DEVICES - 1), jnp.int32(PER_SECTION))
    return levels[step, section]


def mod_row(mod_ref, part, level):
    return mod_ref[pl.ds(part * LEVELS + level, 1), :]


def modulated(values, mod_ref, level):
    normed = layer_norm(values.astype(jnp.float32))
    return (normed * (1.0 + mod_row(mod_ref, 1, level)) + mod_row(mod_ref, 0, level)).astype(jnp.bfloat16)


def prepare(place, levels, mod_ref, around_ref, out_ref, window_ref):
    start = 2 * BAND
    middle = around_ref[start : start + HELD, :]
    partner = around_ref[start + HELD : start + 2 * HELD, :]
    diagonal = around_ref[start + 2 * HELD : start + 3 * HELD, :]
    even = place[1] == 0
    bands = [
        around_ref[:BAND, :],
        jnp.where(even, diagonal, partner),
        middle,
        jnp.where(even, partner, diagonal),
        around_ref[BAND : 2 * BAND, :],
    ]
    for i, band in enumerate(bands):
        level = level_of(levels, 0, place[0] - PER_SECTION + i - 2)
        out_ref[i * BAND : (i + 1) * BAND, :] = modulated(band[:BAND], mod_ref, level)
        if 0 < i < 4:
            window_ref[(i - 1) * HELD : i * HELD, :] = band


def attend(query, key, value, first, bias):
    scores = lax.dot_general(
        query[first : first + BAND],
        key[first : first + 3 * BAND],
        (((1,), (1,)), ((), ())),
        preferred_element_type=jnp.float32,
    )
    scores = scores + bias
    peak = jnp.max(scores, axis=-1, keepdims=True)
    weights = jnp.exp2(scores - peak).astype(jnp.bfloat16)
    mixed = jnp.dot(weights, value[first : first + 3 * BAND], preferred_element_type=jnp.float32)
    return (mixed[:, :HEAD_DIM] / mixed[:, HEAD_DIM:]).astype(jnp.bfloat16)


def bias_row(previous, following):
    lane = lax.broadcasted_iota(jnp.int32, (1, 3 * BAND), 1)
    closed = jnp.where(lane < BAND, previous, jnp.where(lane >= 2 * BAND, following, 0.0))
    return closed * -1e30


def compute(
    place,
    levels,
    bounds,
    mod_ref,
    normed_ref,
    window_ref,
    gain_query_ref,
    gain_key_ref,
    gathered_ref,
    out_ref,
    weights,
    query,
    key,
    value,
    advanced,
    normed,
    gates,
    sem,
):
    frame = place[0]

    def copy_of(tile):
        core, first = divmod(tile * COPY, HALF)
        return pltpu.make_async_copy(
            gathered_ref.at[:, core, :, pl.ds(first, COPY)],
            weights.at[:, :, pl.ds(tile * COPY, COPY)],
            sem.at[tile],
        )

    for tile in range(6):
        copy_of(tile).start()

    def project(source, bands, first_use):
        rows = bands * BAND
        inner = (bands - 2) * BAND

        def folded(product):
            squares = product * product
            return sum(squares[:, i : i + 128] for i in range(0, squares.shape[1], 128))

        def norm(power):
            return lax.rsqrt(jnp.sum(power, axis=-1, keepdims=True) * (1.0 / D) + EPSILON)

        query_power = key_power = 0.0
        for first, end in TILES:
            if first_use:
                for i in range(first // COPY, end // COPY):
                    copy_of(i).wait()
            spot = slice(first % D, (end - 1) % D + 1)
            tile = weights[:, :, first:end].reshape(D, end - first)
            used = source[BAND : BAND + inner, :] if end <= D else source[:rows, :]
            product = jnp.dot(used, tile, preferred_element_type=jnp.float32)
            if end <= D:
                query[:inner, spot] = product
                query_power = query_power + folded(product)
            elif end <= 2 * D:
                key[:rows, spot] = product
                key_power = key_power + folded(product)
            else:
                value[:rows, spot] = product.astype(jnp.bfloat16)
        return norm(query_power), norm(key_power)

    def heads_of(bands, query_norm, key_norm, biases, finish):
        rows = bands * BAND
        inner = (bands - 2) * BAND

        def one_head(h, carry):
            lanes = pl.ds(pl.multiple_of(h * HEAD_DIM, HEAD_DIM), HEAD_DIM)
            head_query = (query[:inner, lanes] * query_norm * (gain_query_ref[:, lanes] * SCALE)).astype(jnp.bfloat16)
            head_key = (key[:rows, lanes] * key_norm * gain_key_ref[:, lanes]).astype(jnp.bfloat16)
            head_value = jnp.concatenate(
                [value[:rows, lanes], jnp.ones((rows, HEAD_DIM), jnp.bfloat16)], axis=1
            )
            for band in range(bands - 2):
                attended = attend(head_query, head_key, head_value, band * BAND, biases[band])
                finish(band, lanes, attended.astype(jnp.float32))
            return carry

        lax.fori_loop(0, HEADS, one_head, 0, unroll=HEADS)

    query_norm, key_norm = project(normed_ref, 5, True)

    biases = []
    for band in range(3):
        flags = window_ref[band * HELD + BAND : (band + 1) * HELD, : 3 * BAND].astype(jnp.float32)
        biases.append(bias_row(flags[0:1], flags[1:2]))

    for band in range(3):
        gates[band : band + 1, :] = mod_row(mod_ref, 2, level_of(levels, 0, frame - PER_SECTION + band - 1))
    gates[3:4, :] = mod_row(mod_ref, 2, level_of(levels, 1, frame))

    def finish_first(band, lanes, attended):
        gate = gates[band : band + 1, lanes]
        held = window_ref[band * HELD : band * HELD + BAND, lanes]
        moved = (held.astype(jnp.float32) + gate * attended).astype(jnp.bfloat16)
        entering = jnp.where(frame + band - 1 < PER_SECTION, held, moved)
        advanced[band * BAND : (band + 1) * BAND, lanes] = entering

    heads_of(5, query_norm, key_norm, biases, finish_first)

    for band in range(3):
        rows = slice(band * BAND, (band + 1) * BAND)
        normed[rows, :] = modulated(advanced[rows, :], mod_ref, level_of(levels, 1, frame + band - 1))

    query_norm, key_norm = project(normed, 3, False)

    bias_second = bias_row(
        jnp.where(bounds[0, 0] >= frame, 1.0, 0.0), jnp.where(bounds[0, 1] <= frame + 1, 1.0, 0.0)
    )

    def finish_second(band, lanes, attended):
        gate = gates[3:4, lanes]
        held = advanced[BAND : 2 * BAND, lanes].astype(jnp.float32)
        out_ref[:, lanes] = (held + gate * attended).astype(jnp.bfloat16)

    heads_of(3, query_norm, key_norm, [bias_second], finish_second)


def prepared(place, levels, table, around):
    smem = pl.BlockSpec(memory_space=pltpu.SMEM)
    vmem = pl.BlockSpec(memory_space=pltpu.VMEM)
    return pl.pallas_call(
        prepare,
        out_shape=[
            jax.ShapeDtypeStruct((5 * BAND, D), jnp.bfloat16),
            jax.ShapeDtypeStruct((3 * HELD, D), jnp.bfloat16),
        ],
        in_specs=[smem] * 2 + [vmem] * 2,
        out_specs=[vmem] * 2,
        compiler_params=pltpu.CompilerParams(vmem_limit_bytes=16 * 1024 * 1024),
        cost_estimate=pl.CostEstimate(flops=10_000_000, bytes_accessed=4_000_000, transcendentals=0),
        name="normed_window",
    )(place, levels, table, around)


def two_steps(place, levels, bounds, table, normed, window, gain_query, gain_key, gathered):
    smem = pl.BlockSpec(memory_space=pltpu.SMEM)
    vmem = pl.BlockSpec(memory_space=pltpu.VMEM)
    anywhere = pl.BlockSpec(memory_space=pl.ANY)
    return pl.pallas_call(
        compute,
        out_shape=jax.ShapeDtypeStruct((BAND, D), jnp.bfloat16),
        in_specs=[smem] * 3 + [vmem] * 5 + [anywhere],
        out_specs=vmem,
        scratch_shapes=[
            pltpu.VMEM((8, 2 * ROWS, 3 * D), jnp.bfloat16),
            pltpu.VMEM((3 * BAND, D), jnp.float32),
            pltpu.VMEM((5 * BAND, D), jnp.float32),
            pltpu.VMEM((5 * BAND, D), jnp.bfloat16),
            pltpu.VMEM((3 * BAND, D), jnp.bfloat16),
            pltpu.VMEM((3 * BAND, D), jnp.bfloat16),
            pltpu.VMEM((8, D), jnp.float32),
            pltpu.SemaphoreType.DMA((6,)),
        ],
        compiler_params=pltpu.CompilerParams(vmem_limit_bytes=48 * 1024 * 1024),
        cost_estimate=pl.CostEstimate(
            flops=12_000_000_000, bytes_accessed=20_000_000, transcendentals=2_000_000
        ),
        name="two_steps",
    )(place, levels, bounds, table, normed, window, gain_query, gain_key, gathered)


def tied(value, *others):
    return lax.optimization_barrier((value, *others))[0]


def shards(
    stream, incoming, levels, bounds, mod_table, w_query, w_key, w_value, gain_query, gain_key
):
    core = lax.axis_index("core")
    frame = lax.axis_index(AXES)
    zh = lax.axis_index("zh")
    place = jnp.stack([frame, zh]).astype(jnp.int32)

    parity = lax.rem(lax.axis_index("x"), 2)
    packed = jnp.concatenate([w_query, w_key, w_value], axis=1)
    half = lax.dynamic_slice_in_dim(packed, core * HALF, HALF, axis=1)
    quarter = lax.dynamic_slice_in_dim(packed, core * HALF + parity * (HALF // 2), HALF // 2, axis=1)
    mirror = [(2 * zl + side, 2 * (3 - zl) + 1 - side) for zl in range(4) for side in range(2)]
    opposite = lax.ppermute(quarter, ("zl", "zh"), mirror)
    ring = [(i, (i + 1) % 4) for i in range(4)]
    beside = [(2 * i, 2 * j) for i, j in ring] + [(2 * j + 1, 2 * i + 1) for i, j in ring]
    neighbour = lax.ppermute(opposite, ("x", "core"), beside)
    row = lax.broadcasted_iota(jnp.int32, (FLAGS, D), 0)
    flags = jnp.where(row == 0, bounds[0, 0] >= frame, bounds[0, 1] <= frame + 1).astype(jnp.bfloat16)
    y = lax.axis_index("y")
    last = frame >= DEVICES - PER_SECTION
    mine = jnp.where(last, incoming, stream)
    flagged = lambda block: jnp.concatenate([block, flags], axis=0)
    held = flagged(mine)

    def moved(block, distance):
        route = [(d, (d + distance) % DEVICES) for d in range(DEVICES)]
        return lax.ppermute(block, AXES, route)

    two_before = moved(mine, 2)
    two_after = moved(jnp.where(last & (y > 0), incoming, stream), -2)
    neighbour = tied(neighbour, two_before, two_after)
    other = jnp.where(
        parity == 0,
        jnp.concatenate([opposite, neighbour], axis=1),
        jnp.concatenate([neighbour, opposite], axis=1),
    )
    both = jnp.where(
        zh == 0, jnp.concatenate([half, other], axis=0), jnp.concatenate([other, half], axis=0)
    )
    gathered = lax.all_gather(both, ("y", "core"), axis=0, tiled=True)

    partner = lax.ppermute(tied(held, opposite), "zh", [(0, 1), (1, 0)])
    diagonal = lax.ppermute(
        tied(flagged(jnp.where(last & (y + zh > 0), incoming, stream)), opposite),
        AXES,
        [(d, (d + 1 if d % 2 else d - 1) % DEVICES) for d in range(DEVICES)],
    )
    around = moved(jnp.concatenate([two_before, two_after, held, partner, diagonal], axis=0), PER_SECTION)

    table = mod_table.transpose(1, 0, 2).reshape(3 * LEVELS, D)
    normed, window = prepared(place, levels, table, around)
    return two_steps(
        place,
        levels,
        bounds,
        table,
        normed,
        window,
        gain_query[None, :],
        gain_key[None, :],
        gathered.reshape(8, 2, 2 * ROWS, HALF),
    )


def solution(mesh):
    inner = Mesh(mesh.devices.reshape(SHAPE), AXES)
    queue_dp = P(AXES, None)
    dp = P(("y", "zh"), None)
    in_specs = (queue_dp, dp, P(), queue_dp, P(), dp, dp, dp, P(), P())
    return jax.shard_map(shards, mesh=inner, in_specs=in_specs, out_specs=queue_dp, check_vma=False)
```

time: 192 us -> 161 us (0.84)
  the two profiles are of different devices: /device:TPU:199 before, /device:TPU:1 now
where the time goes in v3:
time: 161 us; the launch traced here: 160 us
  waiting for transfers between devices  76.5 us (48%)
  starting transfers between devices  40.4 us (25%)
  Pallas kernels  22.2 us (14%)
  between operations  15 us (9%)
  local copies, waits for them, and re-layouts  4.06 us (3%)
    ppermute x1, waiting for transfers between devices, shards(): partner = lax.ppermute(tied(held, opposite), 'zh', [(0, 1), (1, 0)])  27.5 us
    all_gather x1, waiting for transfers between devices, shards(): gathered = lax.all_gather(both, ('y', 'core'), axis=0, tiled=True)  23.3 us
    ppermute x3, waiting for transfers between devices, moved(): return lax.ppermute(block, AXES, route)  20.4 us
    pallas_call x1, Pallas kernels, two_steps(): pl.pallas_call(compute, out_shape=jax.ShapeDtypeStruct((BAND, D), jnp.bfl...  20.4 us
    ppermute x1, starting transfers between devices, shards(): opposite = lax.ppermute(quarter, ('zl', 'zh'), mirror)  11.5 us
    ppermute x1, starting transfers between devices, shards(): lax.ppermute(tied(flagged(jnp.where(last & (y + zh > 0), incoming, stream...  11 us
    ppermute x3, starting transfers between devices, moved(): return lax.ppermute(block, AXES, route)  9.88 us
    ppermute x1, starting transfers between devices, shards(): neighbour = lax.ppermute(opposite, ('x', 'core'), beside)  4.38 us
  transfers between devices with their start and end apart: 8, of which 5 were waited for; matrix products, arithmetic and copies ran while one was open for 1% of the time, Pallas kernels for 1%

profile of v3, /device:TPU:1, one launch (start us, length us, event | category | flops | bytes accessed | tf_op | source)
XLA Modules:
  0.0 159.6 jit_solution(7725452859587111490)
XLA Ops:
  6.5 1.0 constant_dynamic-update-slice_fusion.2
  7.6 1.0 constant_dynamic-update-slice_fusion.1
  8.6 1.0 constant_dynamic-update-slice_fusion
  9.6 11.5 %collective-permute-start.2 = (bf16[96,1152]{1,0:T(8,128)(2,1)S(1)}, bf16[96,1152]{1,0:T(8,128)(2,1)S(1)}, u32[]{:S(2)}, u32[]{:S(2)}) collective-permute-start(bf16[96,1152]{1,0:T(8,128)(2,1)S(1)} %constant_dynamic-slice_fusion.1), channel_id=1, source_target_pairs={{0,385},{1,384},{128,257},{129,256},{256,129},{257,128},{384,1},{3... | collective-permute-start | bytes 663560 | tf_op jit(solution)/shard_map/ppermute | solution.py:269
  21.2 0.1 broadcast_select_fusion
  21.2 3.2 %collective-permute-start = (bf16[112,1536]{1,0:T(8,128)(2,1)S(1)}, bf16[112,1536]{1,0:T(8,128)(2,1)S(1)}, u32[]{:S(2)}, u32[]{:S(2)}) collective-permute-start(bf16[112,1536]{1,0:T(8,128)(2,1)S(1)} %get-tuple-element.16), channel_id=1, source_target_pairs={{0,2},{1,3},{2,4},{3,5},{4,6},{5,7},{6,8},{7,9},{8,10},{9,11},{10,... | collective-permute-start | bytes 1032200 | tf_op jit(solution)/shard_map/ppermute | solution.py:283
  24.5 4.7 %collective-permute-start.1 = (bf16[112,1536]{1,0:T(8,128)(2,1)S(1)}, bf16[112,1536]{1,0:T(8,128)(2,1)S(1)}, u32[]{:S(2)}, u32[]{:S(2)}) collective-permute-start(bf16[112,1536]{1,0:T(8,128)(2,1)S(1)} %get-tuple-element.17), channel_id=1, source_target_pairs={{0,510},{1,511},{2,0},{3,1},{4,2},{5,3},{6,4},{7,5},{8,6},{9,7},{1... | collective-permute-start | bytes 1032200 | tf_op jit(solution)/shard_map/ppermute | solution.py:283
  29.1 2.6 %collective-permute-done.2 = bf16[96,1152]{1,0:T(8,128)(2,1)S(1)} collective-permute-done((bf16[96,1152]{1,0:T(8,128)(2,1)S(1)}, bf16[96,1152]{1,0:T(8,128)(2,1)S(1)}, u32[]{:S(2)}, u32[]{:S(2)}) %collective-permute-start.2) | collective-permute-done | bytes 221216 | tf_op jit(solution)/shard_map/ppermute | solution.py:269
  31.7 4.4 %collective-permute-start.6 = (bf16[96,1152]{1,0:T(8,128)(2,1)S(1)}, bf16[96,1152]{1,0:T(8,128)(2,1)S(1)}, u32[]{:S(2)}, u32[]{:S(2)}) collective-permute-start(bf16[96,1152]{1,0:T(8,128)(2,1)S(1)} %collective-permute-done.2), channel_id=1, source_target_pairs={{0,32},{32,64},{64,96},{96,0},{48,16},{80,48},{112,80},{16,112},{1... | collective-permute-start | bytes 663560 | tf_op jit(solution)/shard_map/ppermute | solution.py:272
  36.2 2.8 %collective-permute-done.6 = bf16[96,1152]{1,0:T(8,128)(2,1)S(1)} collective-permute-done((bf16[96,1152]{1,0:T(8,128)(2,1)S(1)}, bf16[96,1152]{1,0:T(8,128)(2,1)S(1)}, u32[]{:S(2)}, u32[]{:S(2)}) %collective-permute-start.6) | collective-permute-done | bytes 221216 | tf_op jit(solution)/shard_map/ppermute | solution.py:272
  39.0 0.1 maximum_select_fusion.1
  39.1 1.1 maximum_select_fusion
  40.2 0.6 fusion
  42.2 0.1 pad_maximum_fusion
  42.3 3.6 %collective-permute-start.3 = (bf16[128,1536]{1,0:T(8,128)(2,1)S(1)}, bf16[128,1536]{1,0:T(8,128)(2,1)S(1)}, u32[]{:S(2)}, u32[]{:S(2)}) collective-permute-start(bf16[128,1536]{1,0:T(8,128)(2,1)S(1)} %get-tuple-element.10), channel_id=1, source_target_pairs={{0,1},{1,0},{2,3},{3,2},{4,5},{5,4},{6,7},{7,6},{8,9},{9,8},{10,11... | collective-permute-start | bytes 1179656 | tf_op jit(solution)/shard_map/ppermute | solution.py:298
  46.0 11.0 %collective-permute-start.4 = (bf16[128,1536]{1,0:T(8,128)(2,1)S(1)}, bf16[128,1536]{1,0:T(8,128)(2,1)S(1)}, u32[]{:S(2)}, u32[]{:S(2)}) collective-permute-start(bf16[128,1536]{1,0:T(8,128)(2,1)S(1)} %get-tuple-element.11), channel_id=1, source_target_pairs={{0,511},{1,2},{2,1},{3,4},{4,3},{5,6},{6,5},{7,8},{8,7},{9,10},{10... | collective-permute-start | bytes 1179656 | tf_op jit(solution)/shard_map/ppermute | solution.py:299
  57.1 0.1 broadcast_dynamic-update-slice_fusion
  57.2 27.5 %collective-permute-done.3 = bf16[128,1536]{1,0:T(8,128)(2,1)S(1)} collective-permute-done((bf16[128,1536]{1,0:T(8,128)(2,1)S(1)}, bf16[128,1536]{1,0:T(8,128)(2,1)S(1)}, u32[]{:S(2)}, u32[]{:S(2)}) %collective-permute-start.3) | collective-permute-done | bytes 393248 | tf_op jit(solution)/shard_map/ppermute | solution.py:298
  84.7 2.0 %collective-permute-start.5 = (bf16[608,1536]{1,0:T(8,128)(2,1)S(1)}, bf16[608,1536]{1,0:T(8,128)(2,1)S(1)}, u32[]{:S(2)}, u32[]{:S(2)}) collective-permute-start(bf16[608,1536]{1,0:T(8,128)(2,1)S(1)} %constant_dynamic-update-slice_fusion.3), channel_id=1, source_target_pairs={{0,16},{1,17},{2,18},{3,19},{4,20},{5,21},{6,22},{7,23},{8,24},{9,... | collective-permute-start | bytes 5603336 | tf_op jit(solution)/shard_map/ppermute | solution.py:283
  86.8 0.1 pad_add_fusion.place
  86.9 20.4 %collective-permute-done.5.around_ref = bf16[608,1536]{1,0:T(8,128)(2,1)S(1)} collective-permute-done((bf16[608,1536]{1,0:T(8,128)(2,1)S(1)}, bf16[608,1536]{1,0:T(8,128)(2,1)S(1)}, u32[]{:S(2)}, u32[]{:S(2)}) %collective-permute-start.5) | collective-permute-done | bytes 1867808 | tf_op jit(solution)/shard_map/ppermute | solution.py:283
  107.3 1.9 %normed_window.1 = (bf16[560,1536]{1,0:T(8,128)(2,1)S(1)}, bf16[384,1536]{1,0:T(8,128)(2,1)S(1)}) custom-call(s32[2]{0:T(128)S(1)} %pad_add_fusion.place, s32[2,32]{1,0:T(2,128)S(1)} %copy-done.2, f32[96,1536]{1,0:T(8,128)S(1)} %bitcast.8, bf16[608,1536]{1,0:T(8,128)(2,1)S(1)} %collective-permute-done.5.around_ref), custom_call_target="tpu_custom_call" | custom-call | flops 10000000 | bytes 4000000 | tf_op jit(solution)/shard_map/normed_window/pallas_call | solution.py:211
  109.1 23.3 %all-gather.2.cloned.1.call-done = bf16[3072,2304]{1,0:T(8,128)(2,1)} async-done(((bf16[192,2304]{1,0:T(8,128)(2,1)}), bf16[3072,2304]{1,0:T(8,128)(2,1)}) %all-gather.2.cloned.1.call-update) | async-done | bytes 14155792 | tf_op jit(solution)/shard_map/all_gather | solution.py:296
  132.4 20.4 %two_steps.1 = bf16[112,1536]{1,0:T(8,128)(2,1)} custom-call(s32[2]{0:T(128)S(1)} %pad_add_fusion.place, s32[2,32]{1,0:T(2,128)S(1)} %copy-done.2, s32[1,2]{1,0:T(1,128)S(1)} %copy-done.1, f32[96,1536]{1,0:T(8,128)S(1)} %bitcast.9, bf16[560,1536]{1,0:T(8,128)(2,1)S(1)} %get-tuple-element.12.normed_ref, bf16[384,1536]{1,0:T(8,128)(2,1)S(1)} %get-tuple-element.13.window_ref, ...), custom_call_target="tpu_custom_call" | custom-call | flops 12000000000 | bytes 20000000 | tf_op jit(solution)/shard_map/two_steps/pallas_call | solution.py:229
  (30 shorter events, 0.4 us)
Async XLA Ops:
  6.5 14.6 %copy-start.4 = (bf16[112,1536]{1,0:T(8,128)(2,1)S(1)}, bf16[112,1536]{1,0:T(8,128)(2,1)}, u32[]{:S(2)}) copy-start(bf16[112,1536]{1,0:T(8,128)(2,1)} %param.10) | copy-start | bytes 1032196
  6.5 14.6 %copy-start.3 = (bf16[112,1536]{1,0:T(8,128)(2,1)S(1)}, bf16[112,1536]{1,0:T(8,128)(2,1)}, u32[]{:S(2)}) copy-start(bf16[112,1536]{1,0:T(8,128)(2,1)} %param.11) | copy-start | bytes 1032196
  6.5 125.9 %all-gather.2.cloned.1.call-start = ((), (), s32[]{:S(2)}) async-start(), calls=%async_computation | async-start | bytes 15040512 | tf_op jit(solution)/shard_map/all_gather | solution.py:296
  9.6 22.1 %collective-permute-start.2 = (bf16[96,1152]{1,0:T(8,128)(2,1)S(1)}, bf16[96,1152]{1,0:T(8,128)(2,1)S(1)}, u32[]{:S(2)}, u32[]{:S(2)}) collective-permute-start(bf16[96,1152]{1,0:T(8,128)(2,1)S(1)} %constant_dynamic-slice_fusion.1), channel_id=1, source_target_pairs={{0,385},{1,384},{128,257},{129,256},{256,129},{257,128},{384,1},{3... | collective-permute-start | bytes 663560 | tf_op jit(solution)/shard_map/ppermute | solution.py:269
  21.2 14.9 %collective-permute-start = (bf16[112,1536]{1,0:T(8,128)(2,1)S(1)}, bf16[112,1536]{1,0:T(8,128)(2,1)S(1)}, u32[]{:S(2)}, u32[]{:S(2)}) collective-permute-start(bf16[112,1536]{1,0:T(8,128)(2,1)S(1)} %get-tuple-element.16), channel_id=1, source_target_pairs={{0,2},{1,3},{2,4},{3,5},{4,6},{5,7},{6,8},{7,9},{8,10},{9,11},{10,... | collective-permute-start | bytes 1032200 | tf_op jit(solution)/shard_map/ppermute | solution.py:283
  24.5 11.7 %collective-permute-start.1 = (bf16[112,1536]{1,0:T(8,128)(2,1)S(1)}, bf16[112,1536]{1,0:T(8,128)(2,1)S(1)}, u32[]{:S(2)}, u32[]{:S(2)}) collective-permute-start(bf16[112,1536]{1,0:T(8,128)(2,1)S(1)} %get-tuple-element.17), channel_id=1, source_target_pairs={{0,510},{1,511},{2,0},{3,1},{4,2},{5,3},{6,4},{7,5},{8,6},{9,7},{1... | collective-permute-start | bytes 1032200 | tf_op jit(solution)/shard_map/ppermute | solution.py:283
  31.7 7.2 %collective-permute-start.6 = (bf16[96,1152]{1,0:T(8,128)(2,1)S(1)}, bf16[96,1152]{1,0:T(8,128)(2,1)S(1)}, u32[]{:S(2)}, u32[]{:S(2)}) collective-permute-start(bf16[96,1152]{1,0:T(8,128)(2,1)S(1)} %collective-permute-done.2), channel_id=1, source_target_pairs={{0,32},{32,64},{64,96},{96,0},{48,16},{80,48},{112,80},{16,112},{1... | collective-permute-start | bytes 663560 | tf_op jit(solution)/shard_map/ppermute | solution.py:272
  36.2 4.0 %copy-start.1 = (s32[1,2]{1,0:T(1,128)S(1)}, s32[1,2]{1,0:T(1,128)}, u32[]{:S(2)}) copy-start(s32[1,2]{1,0:T(1,128)} %bounds.1) | copy-start | bytes 28
  42.3 44.5 %copy-start.5 = (f32[1536]{0:T(1024)S(1)}, f32[1536]{0:T(1024)}, u32[]{:S(2)}) copy-start(f32[1536]{0:T(1024)} %param.18) | copy-start | bytes 18436
  42.3 44.5 %copy-start.6 = (f32[1536]{0:T(1024)S(1)}, f32[1536]{0:T(1024)}, u32[]{:S(2)}) copy-start(f32[1536]{0:T(1024)} %param.19) | copy-start | bytes 18436
  42.3 65.0 %copy-start = (f32[32,3,1536]{2,0,1:T(8,128)S(1)}, f32[32,3,1536]{2,0,1:T(8,128)}, u32[]{:S(2)}) copy-start(f32[32,3,1536]{2,0,1:T(8,128)} %param.14) | copy-start | bytes 1769476
  42.3 64.9 %copy-start.2 = (s32[2,32]{1,0:T(2,128)S(1)}, s32[2,32]{1,0:T(2,128)}, u32[]{:S(2)}) copy-start(s32[2,32]{1,0:T(2,128)} %levels.3) | copy-start | bytes 772
  42.3 42.3 %collective-permute-start.3 = (bf16[128,1536]{1,0:T(8,128)(2,1)S(1)}, bf16[128,1536]{1,0:T(8,128)(2,1)S(1)}, u32[]{:S(2)}, u32[]{:S(2)}) collective-permute-start(bf16[128,1536]{1,0:T(8,128)(2,1)S(1)} %get-tuple-element.10), channel_id=1, source_target_pairs={{0,1},{1,0},{2,3},{3,2},{4,5},{5,4},{6,7},{7,6},{8,9},{9,8},{10,11... | collective-permute-start | bytes 1179656 | tf_op jit(solution)/shard_map/ppermute | solution.py:298
  46.0 38.7 %collective-permute-start.4 = (bf16[128,1536]{1,0:T(8,128)(2,1)S(1)}, bf16[128,1536]{1,0:T(8,128)(2,1)S(1)}, u32[]{:S(2)}, u32[]{:S(2)}) collective-permute-start(bf16[128,1536]{1,0:T(8,128)(2,1)S(1)} %get-tuple-element.11), channel_id=1, source_target_pairs={{0,511},{1,2},{2,1},{3,4},{4,3},{5,6},{6,5},{7,8},{8,7},{9,10},{10... | collective-permute-start | bytes 1179656 | tf_op jit(solution)/shard_map/ppermute | solution.py:299
  84.7 22.5 %collective-permute-start.5 = (bf16[608,1536]{1,0:T(8,128)(2,1)S(1)}, bf16[608,1536]{1,0:T(8,128)(2,1)S(1)}, u32[]{:S(2)}, u32[]{:S(2)}) collective-permute-start(bf16[608,1536]{1,0:T(8,128)(2,1)S(1)} %constant_dynamic-update-slice_fusion.3), channel_id=1, source_target_pairs={{0,16},{1,17},{2,18},{3,19},{4,20},{5,21},{6,22},{7,23},{8,24},{9,... | collective-permute-start | bytes 5603336 | tf_op jit(solution)/shard_map/ppermute | solution.py:283
Sparse Core Ops, SparseCore 0:
  40.3 92.0 all-gather.1

commit v4 on v3

--- a/solution.py
+++ b/solution.py
@@ -16,7 +16,7 @@
 ROWS = D // PER_SECTION
 HALF = 3 * D // 2
 COPY = 768
-TILES = ((0, 768), (768, 1536), (1536, 2304), (2304, 3072), (3072, 4608))
+TILES = ((0, 768), (768, 1536), (1536, 3072), (3072, 4608))
 FLAGS = 16
 HELD = BAND + FLAGS
 EPSILON = 1e-06
@@ -47,17 +47,17 @@
 
 
 def prepare(place, levels, mod_ref, around_ref, out_ref, window_ref):
-    start = 2 * BAND
+    start = 2 * HELD
     middle = around_ref[start : start + HELD, :]
     partner = around_ref[start + HELD : start + 2 * HELD, :]
     diagonal = around_ref[start + 2 * HELD : start + 3 * HELD, :]
     even = place[1] == 0
     bands = [
-        around_ref[:BAND, :],
+        around_ref[:HELD, :],
         jnp.where(even, diagonal, partner),
         middle,
         jnp.where(even, partner, diagonal),
-        around_ref[BAND : 2 * BAND, :],
+        around_ref[HELD : 2 * HELD, :],
     ]
     for i, band in enumerate(bands):
         level = level_of(levels, 0, place[0] - PER_SECTION + i - 2)
@@ -282,8 +282,8 @@
         route = [(d, (d + distance) % DEVICES) for d in range(DEVICES)]
         return lax.ppermute(block, AXES, route)
 
-    two_before = moved(mine, 2)
-    two_after = moved(jnp.where(last & (y > 0), incoming, stream), -2)
+    two_before = moved(held, 2)
+    two_after = moved(flagged(jnp.where(last & (y > 0), incoming, stream)), -2)
     neighbour = tied(neighbour, two_before, two_after)
     other = jnp.where(
         parity == 0,
@@ -295,13 +295,9 @@
     )
     gathered = lax.all_gather(both, ("y", "core"), axis=0, tiled=True)
 
-    partner = lax.ppermute(tied(held, opposite), "zh", [(0, 1), (1, 0)])
-    diagonal = lax.ppermute(
-        tied(flagged(jnp.where(last & (y + zh > 0), incoming, stream)), opposite),
-        AXES,
-        [(d, (d + 1 if d % 2 else d - 1) % DEVICES) for d in range(DEVICES)],
-    )
-    around = moved(jnp.concatenate([two_before, two_after, held, partner, diagonal], axis=0), PER_SECTION)
+    given = jnp.concatenate([held, jnp.where(zh == 1, two_before, two_after)], axis=0)
+    taken = lax.ppermute(tied(given, opposite), "zh", [(0, 1), (1, 0)])
+    around = moved(jnp.concatenate([two_before, two_after, held, taken], axis=0), PER_SECTION)
 
     table = mod_table.transpose(1, 0, 2).reshape(3 * LEVELS, D)
     normed, window = prepared(place, levels, table, around)

time: 161 us -> 151 us (0.938)
  starting transfers between devices: 40.4 us -> 31.4 us
  waiting for transfers between devices: 76.5 us -> 78.3 us
    ppermute x2 -> x1, starting transfers between devices: 14.7 us -> 3.59 us  [shards(): taken = lax.ppermute(tied(given, opposite), 'zh', [(0, 1), (1, 0)])]
    ppermute x2 -> x1, waiting for transfers between devices: 27.5 us -> 33.3 us  [shards(): taken = lax.ppermute(tied(given, opposite), 'zh', [(0, 1), (1, 0)])]
    ppermute x3, waiting for transfers between devices: 20.4 us -> 24.2 us  [moved(): return lax.ppermute(block, AXES, route)]
    all_gather x1, waiting for transfers between devices: 23.3 us -> 20 us  [shards(): gathered = lax.all_gather(both, ('y', 'core'), axis=0, tiled=True)]
    ppermute x1, waiting for transfers between devices: 2.78 us -> 0.01 us  [shards(): neighbour = lax.ppermute(opposite, ('x', 'core'), beside)]
    ppermute x3, starting transfers between devices: 9.88 us -> 11.9 us  [moved(): return lax.ppermute(block, AXES, route)]
    ppermute x1, waiting for transfers between devices: 2.6 us -> 0.65 us  [shards(): opposite = lax.ppermute(quarter, ('zl', 'zh'), mirror)]
  transfers between devices with their start and end apart: 8 -> 7, of which waited for: 5 -> 5; matrix products, arithmetic and copies ran while one was open for 1% -> 1% of each run, Pallas kernels for 1% -> 1%
where the time goes in v4:
time: 151 us
  waiting for transfers between devices  78.3 us (52%)
  starting transfers between devices  31.4 us (21%)
  Pallas kernels  21 us (14%)
  between operations  14.9 us (10%)
  local copies, waits for them, and re-layouts  3.98 us (3%)
  other arithmetic  1.57 us (1%)
    ppermute x1, waiting for transfers between devices, shards(): taken = lax.ppermute(tied(given, opposite), 'zh', [(0, 1), (1, 0)])  33.3 us
    ppermute x3, waiting for transfers between devices, moved(): return lax.ppermute(block, AXES, route)  24.2 us
    all_gather x1, waiting for transfers between devices, shards(): gathered = lax.all_gather(both, ('y', 'core'), axis=0, tiled=True)  20 us
    pallas_call x1, Pallas kernels, two_steps(): pl.pallas_call(compute, out_shape=jax.ShapeDtypeStruct((BAND, D), jnp.bfl...  19.1 us
    ppermute x3, starting transfers between devices, moved(): return lax.ppermute(block, AXES, route)  11.9 us
    ppermute x1, starting transfers between devices, shards(): opposite = lax.ppermute(quarter, ('zl', 'zh'), mirror)  11.5 us
    ppermute x1, starting transfers between devices, shards(): neighbour = lax.ppermute(opposite, ('x', 'core'), beside)  4.38 us
    ppermute x1, starting transfers between devices, shards(): taken = lax.ppermute(tied(given, opposite), 'zh', [(0, 1), (1, 0)])  3.59 us
  transfers between devices with their start and end apart: 7, of which 5 were waited for; matrix products, arithmetic and copies ran while one was open for 1% of the time, Pallas kernels for 1%

profile of v4, /device:TPU:1, one launch (start us, length us, event | category | flops | bytes accessed | tf_op | source)
XLA Modules:
  0.0 151.1 jit_solution(8491865343399283535)
XLA Ops:
  6.5 1.0 constant_dynamic-update-slice_fusion.2
  7.6 1.0 constant_dynamic-update-slice_fusion.1
  8.6 1.0 constant_dynamic-update-slice_fusion
  9.6 11.5 %collective-permute-start.2 = (bf16[96,1152]{1,0:T(8,128)(2,1)S(1)}, bf16[96,1152]{1,0:T(8,128)(2,1)S(1)}, u32[]{:S(2)}, u32[]{:S(2)}) collective-permute-start(bf16[96,1152]{1,0:T(8,128)(2,1)S(1)} %constant_dynamic-slice_fusion.1), channel_id=1, source_target_pairs={{0,385},{1,384},{128,257},{129,256},{256,129},{257,128},{384,1},{3... | collective-permute-start | bytes 663560 | tf_op jit(solution)/shard_map/ppermute | solution.py:269
  21.1 0.6 fusion
  23.0 0.1 iota.7
  23.1 0.1 pad_maximum_fusion.1
  23.2 3.2 %collective-permute-start = (bf16[128,1536]{1,0:T(8,128)(2,1)S(1)}, bf16[128,1536]{1,0:T(8,128)(2,1)S(1)}, u32[]{:S(2)}, u32[]{:S(2)}) collective-permute-start(bf16[128,1536]{1,0:T(8,128)(2,1)S(1)} %get-tuple-element.18), channel_id=1, source_target_pairs={{0,2},{1,3},{2,4},{3,5},{4,6},{5,7},{6,8},{7,9},{8,10},{9,11},{10,... | collective-permute-start | bytes 1179656 | tf_op jit(solution)/shard_map/ppermute | solution.py:283
  26.4 4.7 %collective-permute-start.1 = (bf16[128,1536]{1,0:T(8,128)(2,1)S(1)}, bf16[128,1536]{1,0:T(8,128)(2,1)S(1)}, u32[]{:S(2)}, u32[]{:S(2)}) collective-permute-start(bf16[128,1536]{1,0:T(8,128)(2,1)S(1)} %get-tuple-element.17), channel_id=1, source_target_pairs={{0,510},{1,511},{2,0},{3,1},{4,2},{5,3},{6,4},{7,5},{8,6},{9,7},{1... | collective-permute-start | bytes 1179656 | tf_op jit(solution)/shard_map/ppermute | solution.py:283
  31.1 0.7 collective-permute-done.2
  31.7 4.4 %collective-permute-start.5 = (bf16[96,1152]{1,0:T(8,128)(2,1)S(1)}, bf16[96,1152]{1,0:T(8,128)(2,1)S(1)}, u32[]{:S(2)}, u32[]{:S(2)}) collective-permute-start(bf16[96,1152]{1,0:T(8,128)(2,1)S(1)} %collective-permute-done.2), channel_id=1, source_target_pairs={{0,32},{32,64},{64,96},{96,0},{48,16},{80,48},{112,80},{16,112},{1... | collective-permute-start | bytes 663560 | tf_op jit(solution)/shard_map/ppermute | solution.py:272
  36.2 2.8 %collective-permute-done = bf16[128,1536]{1,0:T(8,128)(2,1)S(1)} collective-permute-done((bf16[128,1536]{1,0:T(8,128)(2,1)S(1)}, bf16[128,1536]{1,0:T(8,128)(2,1)S(1)}, u32[]{:S(2)}, u32[]{:S(2)}) %collective-permute-start) | collective-permute-done | bytes 393248 | tf_op jit(solution)/shard_map/ppermute | solution.py:283
  39.0 0.1 maximum_select_fusion.1
  39.1 1.1 maximum_select_fusion
  40.2 0.1 broadcast_select_fusion
  40.5 3.6 %collective-permute-start.3 = (bf16[256,1536]{1,0:T(8,128)(2,1)S(1)}, bf16[256,1536]{1,0:T(8,128)(2,1)S(1)}, u32[]{:S(2)}, u32[]{:S(2)}) collective-permute-start(bf16[256,1536]{1,0:T(8,128)(2,1)S(1)} %pad_maximum_fusion), channel_id=1, source_target_pairs={{0,1},{1,0},{2,3},{3,2},{4,5},{5,4},{6,7},{7,6},{8,9},{9,8},{10,11... | collective-permute-start | bytes 2359304 | tf_op jit(solution)/shard_map/ppermute | solution.py:299
  44.1 0.1 broadcast_dynamic-update-slice_fusion
  44.2 33.3 %collective-permute-done.3 = bf16[256,1536]{1,0:T(8,128)(2,1)S(1)} collective-permute-done((bf16[256,1536]{1,0:T(8,128)(2,1)S(1)}, bf16[256,1536]{1,0:T(8,128)(2,1)S(1)}, u32[]{:S(2)}, u32[]{:S(2)}) %collective-permute-start.3) | collective-permute-done | bytes 786464 | tf_op jit(solution)/shard_map/ppermute | solution.py:299
  77.6 4.1 %collective-permute-start.4 = (bf16[640,1536]{1,0:T(8,128)(2,1)S(1)}, bf16[640,1536]{1,0:T(8,128)(2,1)S(1)}, u32[]{:S(2)}, u32[]{:S(2)}) collective-permute-start(bf16[640,1536]{1,0:T(8,128)(2,1)S(1)} %constant_dynamic-update-slice_fusion.3), channel_id=1, source_target_pairs={{0,16},{1,17},{2,18},{3,19},{4,20},{5,21},{6,22},{7,23},{8,24},{9,... | collective-permute-start | bytes 5898248 | tf_op jit(solution)/shard_map/ppermute | solution.py:283
  81.7 0.1 pad_add_fusion.place
  81.8 21.4 %collective-permute-done.4.around_ref = bf16[640,1536]{1,0:T(8,128)(2,1)S(1)} collective-permute-done((bf16[640,1536]{1,0:T(8,128)(2,1)S(1)}, bf16[640,1536]{1,0:T(8,128)(2,1)S(1)}, u32[]{:S(2)}, u32[]{:S(2)}) %collective-permute-start.4) | collective-permute-done | bytes 1966112 | tf_op jit(solution)/shard_map/ppermute | solution.py:283
  103.2 1.9 %normed_window.1 = (bf16[560,1536]{1,0:T(8,128)(2,1)S(1)}, bf16[384,1536]{1,0:T(8,128)(2,1)S(1)}) custom-call(s32[2]{0:T(128)S(1)} %pad_add_fusion.place, s32[2,32]{1,0:T(2,128)S(1)} %copy-done.2, f32[96,1536]{1,0:T(8,128)S(1)} %bitcast.8, bf16[640,1536]{1,0:T(8,128)(2,1)S(1)} %collective-permute-done.4.around_ref), custom_call_target="tpu_custom_call" | custom-call | flops 10000000 | bytes 4000000 | tf_op jit(solution)/shard_map/normed_window/pallas_call | solution.py:211
  105.1 20.0 %all-gather.2.cloned.1.call-done = bf16[3072,2304]{1,0:T(8,128)(2,1)} async-done(((bf16[192,2304]{1,0:T(8,128)(2,1)}), bf16[3072,2304]{1,0:T(8,128)(2,1)}) %all-gather.2.cloned.1.call-update) | async-done | bytes 14155792 | tf_op jit(solution)/shard_map/all_gather | solution.py:296
  125.1 19.1 %two_steps.1 = bf16[112,1536]{1,0:T(8,128)(2,1)} custom-call(s32[2]{0:T(128)S(1)} %pad_add_fusion.place, s32[2,32]{1,0:T(2,128)S(1)} %copy-done.2, s32[1,2]{1,0:T(1,128)S(1)} %copy-done.1, f32[96,1536]{1,0:T(8,128)S(1)} %bitcast.9, bf16[560,1536]{1,0:T(8,128)(2,1)S(1)} %get-tuple-element.10.normed_ref, bf16[384,1536]{1,0:T(8,128)(2,1)S(1)} %get-tuple-element.11.window_ref, ...), custom_call_target="tpu_custom_call" | custom-call | flops 12000000000 | bytes 20000000 | tf_op jit(solution)/shard_map/two_steps/pallas_call | solution.py:229
  (28 shorter events, 0.4 us)
Async XLA Ops:
  6.5 14.6 %copy-start.1 = (s32[1,2]{1,0:T(1,128)S(1)}, s32[1,2]{1,0:T(1,128)}, u32[]{:S(2)}) copy-start(s32[1,2]{1,0:T(1,128)} %bounds.1) | copy-start | bytes 28
  6.5 16.4 %copy-start.4 = (bf16[112,1536]{1,0:T(8,128)(2,1)S(1)}, bf16[112,1536]{1,0:T(8,128)(2,1)}, u32[]{:S(2)}) copy-start(bf16[112,1536]{1,0:T(8,128)(2,1)} %param.10) | copy-start | bytes 1032196
  6.5 16.4 %copy-start.3 = (bf16[112,1536]{1,0:T(8,128)(2,1)S(1)}, bf16[112,1536]{1,0:T(8,128)(2,1)}, u32[]{:S(2)}) copy-start(bf16[112,1536]{1,0:T(8,128)(2,1)} %param.11) | copy-start | bytes 1032196
  6.5 118.5 %all-gather.2.cloned.1.call-start = ((), (), s32[]{:S(2)}) async-start(), calls=%async_computation | async-start | bytes 15040512 | tf_op jit(solution)/shard_map/all_gather | solution.py:296
  9.6 22.1 %collective-permute-start.2 = (bf16[96,1152]{1,0:T(8,128)(2,1)S(1)}, bf16[96,1152]{1,0:T(8,128)(2,1)S(1)}, u32[]{:S(2)}, u32[]{:S(2)}) collective-permute-start(bf16[96,1152]{1,0:T(8,128)(2,1)S(1)} %constant_dynamic-slice_fusion.1), channel_id=1, source_target_pairs={{0,385},{1,384},{128,257},{129,256},{256,129},{257,128},{384,1},{3... | collective-permute-start | bytes 663560 | tf_op jit(solution)/shard_map/ppermute | solution.py:269
  23.2 15.8 %collective-permute-start = (bf16[128,1536]{1,0:T(8,128)(2,1)S(1)}, bf16[128,1536]{1,0:T(8,128)(2,1)S(1)}, u32[]{:S(2)}, u32[]{:S(2)}) collective-permute-start(bf16[128,1536]{1,0:T(8,128)(2,1)S(1)} %get-tuple-element.18), channel_id=1, source_target_pairs={{0,2},{1,3},{2,4},{3,5},{4,6},{5,7},{6,8},{7,9},{8,10},{9,11},{10,... | collective-permute-start | bytes 1179656 | tf_op jit(solution)/shard_map/ppermute | solution.py:283
  26.4 12.6 %collective-permute-start.1 = (bf16[128,1536]{1,0:T(8,128)(2,1)S(1)}, bf16[128,1536]{1,0:T(8,128)(2,1)S(1)}, u32[]{:S(2)}, u32[]{:S(2)}) collective-permute-start(bf16[128,1536]{1,0:T(8,128)(2,1)S(1)} %get-tuple-element.17), channel_id=1, source_target_pairs={{0,510},{1,511},{2,0},{3,1},{4,2},{5,3},{6,4},{7,5},{8,6},{9,7},{1... | collective-permute-start | bytes 1179656 | tf_op jit(solution)/shard_map/ppermute | solution.py:283
  31.7 7.3 %collective-permute-start.5 = (bf16[96,1152]{1,0:T(8,128)(2,1)S(1)}, bf16[96,1152]{1,0:T(8,128)(2,1)S(1)}, u32[]{:S(2)}, u32[]{:S(2)}) collective-permute-start(bf16[96,1152]{1,0:T(8,128)(2,1)S(1)} %collective-permute-done.2), channel_id=1, source_target_pairs={{0,32},{32,64},{64,96},{96,0},{48,16},{80,48},{112,80},{16,112},{1... | collective-permute-start | bytes 663560 | tf_op jit(solution)/shard_map/ppermute | solution.py:272
  40.4 41.3 %copy-start.5 = (f32[1536]{0:T(1024)S(1)}, f32[1536]{0:T(1024)}, u32[]{:S(2)}) copy-start(f32[1536]{0:T(1024)} %param.18) | copy-start | bytes 18436
  40.4 41.3 %copy-start.6 = (f32[1536]{0:T(1024)S(1)}, f32[1536]{0:T(1024)}, u32[]{:S(2)}) copy-start(f32[1536]{0:T(1024)} %param.19) | copy-start | bytes 18436
  40.4 62.8 %copy-start = (f32[32,3,1536]{2,0,1:T(8,128)S(1)}, f32[32,3,1536]{2,0,1:T(8,128)}, u32[]{:S(2)}) copy-start(f32[32,3,1536]{2,0,1:T(8,128)} %param.14) | copy-start | bytes 1769476
  40.4 62.8 %copy-start.2 = (s32[2,32]{1,0:T(2,128)S(1)}, s32[2,32]{1,0:T(2,128)}, u32[]{:S(2)}) copy-start(s32[2,32]{1,0:T(2,128)} %levels.3) | copy-start | bytes 772
  40.5 37.1 %collective-permute-start.3 = (bf16[256,1536]{1,0:T(8,128)(2,1)S(1)}, bf16[256,1536]{1,0:T(8,128)(2,1)S(1)}, u32[]{:S(2)}, u32[]{:S(2)}) collective-permute-start(bf16[256,1536]{1,0:T(8,128)(2,1)S(1)} %pad_maximum_fusion), channel_id=1, source_target_pairs={{0,1},{1,0},{2,3},{3,2},{4,5},{5,4},{6,7},{7,6},{8,9},{9,8},{10,11... | collective-permute-start | bytes 2359304 | tf_op jit(solution)/shard_map/ppermute | solution.py:299
  77.6 25.6 %collective-permute-start.4 = (bf16[640,1536]{1,0:T(8,128)(2,1)S(1)}, bf16[640,1536]{1,0:T(8,128)(2,1)S(1)}, u32[]{:S(2)}, u32[]{:S(2)}) collective-permute-start(bf16[640,1536]{1,0:T(8,128)(2,1)S(1)} %constant_dynamic-update-slice_fusion.3), channel_id=1, source_target_pairs={{0,16},{1,17},{2,18},{3,19},{4,20},{5,21},{6,22},{7,23},{8,24},{9,... | collective-permute-start | bytes 5898248 | tf_op jit(solution)/shard_map/ppermute | solution.py:283
Sparse Core Ops, SparseCore 0:
  40.3 84.7 all-gather.1

commit v5 on v4

--- a/solution.py
+++ b/solution.py
@@ -262,14 +262,18 @@
     place = jnp.stack([frame, zh]).astype(jnp.int32)
 
     parity = lax.rem(lax.axis_index("x"), 2)
-    packed = jnp.concatenate([w_query, w_key, w_value], axis=1)
-    half = lax.dynamic_slice_in_dim(packed, core * HALF, HALF, axis=1)
-    quarter = lax.dynamic_slice_in_dim(packed, core * HALF + parity * (HALF // 2), HALF // 2, axis=1)
+    half = jnp.where(
+        core == 0,
+        jnp.concatenate([w_query, w_key[:, : HALF - D]], axis=1),
+        jnp.concatenate([w_key[:, HALF - D :], w_value], axis=1),
+    )
+    quarter = lax.dynamic_slice_in_dim(tied(half), parity * (HALF // 2), HALF // 2, axis=1)
     mirror = [(2 * zl + side, 2 * (3 - zl) + 1 - side) for zl in range(4) for side in range(2)]
     opposite = lax.ppermute(quarter, ("zl", "zh"), mirror)
     ring = [(i, (i + 1) % 4) for i in range(4)]
     beside = [(2 * i, 2 * j) for i, j in ring] + [(2 * j + 1, 2 * i + 1) for i, j in ring]
     neighbour = lax.ppermute(opposite, ("x", "core"), beside)
+    stream, incoming, bounds = lax.optimization_barrier((stream, incoming, bounds, quarter))[:3]
     row = lax.broadcasted_iota(jnp.int32, (FLAGS, D), 0)
     flags = jnp.where(row == 0, bounds[0, 0] >= frame, bounds[0, 1] <= frame + 1).astype(jnp.bfloat16)
     y = lax.axis_index("y")

time: 151 us -> 151 us (level)
  starting transfers between devices: 31.4 us -> 38.9 us
  waiting for transfers between devices: 78.3 us -> 70.8 us
  local copies, waits for them, and re-layouts: 3.98 us -> 2.02 us
    ppermute x3, starting transfers between devices: 11.9 us -> 19.5 us  [moved(): return lax.ppermute(block, AXES, route)]
    all_gather x1, waiting for transfers between devices: 20 us -> 15.6 us  [shards(): gathered = lax.all_gather(both, ('y', 'core'), axis=0, tiled=True)]
    ppermute x1, waiting for transfers between devices: 33.3 us -> 30.2 us  [shards(): taken = lax.ppermute(tied(given, opposite), 'zh', [(0, 1), (1, 0)])]
    unnamed x19 -> x17, local copies, waits for them, and re-layouts: 2.2 us -> 0.16 us
where the time goes in v5:
time: 151 us; the launch traced here: 150 us
  waiting for transfers between devices  70.8 us (47%)
  starting transfers between devices  38.9 us (26%)
  Pallas kernels  21 us (14%)
  between operations  14.9 us (10%)
  other arithmetic  2.72 us (2%)
  local copies, waits for them, and re-layouts  2.02 us (1%)
    ppermute x1, waiting for transfers between devices, shards(): taken = lax.ppermute(tied(given, opposite), 'zh', [(0, 1), (1, 0)])  30.2 us
    ppermute x3, waiting for transfers between devices, moved(): return lax.ppermute(block, AXES, route)  24.4 us
    ppermute x3, starting transfers between devices, moved(): return lax.ppermute(block, AXES, route)  19.5 us
    pallas_call x1, Pallas kernels, two_steps(): pl.pallas_call(compute, out_shape=jax.ShapeDtypeStruct((BAND, D), jnp.bfl...  19.1 us
    all_gather x1, waiting for transfers between devices, shards(): gathered = lax.all_gather(both, ('y', 'core'), axis=0, tiled=True)  15.6 us
    ppermute x1, starting transfers between devices, shards(): opposite = lax.ppermute(quarter, ('zl', 'zh'), mirror)  11.5 us
    ppermute x1, starting transfers between devices, shards(): neighbour = lax.ppermute(opposite, ('x', 'core'), beside)  4.38 us
    ppermute x1, starting transfers between devices, shards(): taken = lax.ppermute(tied(given, opposite), 'zh', [(0, 1), (1, 0)])  3.5 us
  transfers between devices with their start and end apart: 7, of which 5 were waited for; matrix products, arithmetic and copies ran while one was open for 1% of the time, Pallas kernels for 1%

profile of v5, /device:TPU:1, one launch (start us, length us, event | category | flops | bytes accessed | tf_op | source)
XLA Modules:
  0.0 150.3 jit_solution(15290280747419687402)
XLA Ops:
  6.5 1.1 fusion
  7.6 1.2 maximum_select_fusion.1
  8.8 11.5 %collective-permute-start.2 = (bf16[96,1152]{1,0:T(8,128)(2,1)S(1)}, bf16[96,1152]{1,0:T(8,128)(2,1)S(1)}, u32[]{:S(2)}, u32[]{:S(2)}) collective-permute-start(bf16[96,1152]{1,0:T(8,128)(2,1)S(1)} %constant_dynamic-slice_fusion), channel_id=1, source_target_pairs={{0,385},{1,384},{128,257},{129,256},{256,129},{257,128},{384,1},{3... | collective-permute-start | bytes 663560 | tf_op jit(solution)/shard_map/ppermute | solution.py:272
  20.4 0.6 fusion.1
  22.3 0.1 iota.7
  22.4 0.1 pad_maximum_fusion.1
  22.5 3.2 %collective-permute-start = (bf16[128,1536]{1,0:T(8,128)(2,1)S(1)}, bf16[128,1536]{1,0:T(8,128)(2,1)S(1)}, u32[]{:S(2)}, u32[]{:S(2)}) collective-permute-start(bf16[128,1536]{1,0:T(8,128)(2,1)S(1)} %get-tuple-element.26), channel_id=1, source_target_pairs={{0,2},{1,3},{2,4},{3,5},{4,6},{5,7},{6,8},{7,9},{8,10},{9,11},{10,... | collective-permute-start | bytes 1179656 | tf_op jit(solution)/shard_map/ppermute | solution.py:287
  25.7 4.7 %collective-permute-start.1 = (bf16[128,1536]{1,0:T(8,128)(2,1)S(1)}, bf16[128,1536]{1,0:T(8,128)(2,1)S(1)}, u32[]{:S(2)}, u32[]{:S(2)}) collective-permute-start(bf16[128,1536]{1,0:T(8,128)(2,1)S(1)} %get-tuple-element.25), channel_id=1, source_target_pairs={{0,510},{1,511},{2,0},{3,1},{4,2},{5,3},{6,4},{7,5},{8,6},{9,7},{1... | collective-permute-start | bytes 1179656 | tf_op jit(solution)/shard_map/ppermute | solution.py:287
  30.4 0.6 collective-permute-done.2
  30.9 4.4 %collective-permute-start.5 = (bf16[96,1152]{1,0:T(8,128)(2,1)S(1)}, bf16[96,1152]{1,0:T(8,128)(2,1)S(1)}, u32[]{:S(2)}, u32[]{:S(2)}) collective-permute-start(bf16[96,1152]{1,0:T(8,128)(2,1)S(1)} %collective-permute-done.2), channel_id=1, source_target_pairs={{0,32},{32,64},{64,96},{96,0},{48,16},{80,48},{112,80},{16,112},{1... | collective-permute-start | bytes 663560 | tf_op jit(solution)/shard_map/ppermute | solution.py:275
  35.3 2.9 %collective-permute-done = bf16[128,1536]{1,0:T(8,128)(2,1)S(1)} collective-permute-done((bf16[128,1536]{1,0:T(8,128)(2,1)S(1)}, bf16[128,1536]{1,0:T(8,128)(2,1)S(1)}, u32[]{:S(2)}, u32[]{:S(2)}) %collective-permute-start) | collective-permute-done | bytes 393248 | tf_op jit(solution)/shard_map/ppermute | solution.py:287
  38.3 0.1 maximum_select_fusion.2
  38.4 1.1 maximum_select_fusion
  39.5 0.1 broadcast_select_fusion
  39.7 0.1 pad_maximum_fusion
  39.8 3.5 %collective-permute-start.3 = (bf16[256,1536]{1,0:T(8,128)(2,1)S(1)}, bf16[256,1536]{1,0:T(8,128)(2,1)S(1)}, u32[]{:S(2)}, u32[]{:S(2)}) collective-permute-start(bf16[256,1536]{1,0:T(8,128)(2,1)S(1)} %pad_maximum_fusion), channel_id=1, source_target_pairs={{0,1},{1,0},{2,3},{3,2},{4,5},{5,4},{6,7},{7,6},{8,9},{9,8},{10,11... | collective-permute-start | bytes 2359304 | tf_op jit(solution)/shard_map/ppermute | solution.py:303
  43.3 0.1 broadcast_dynamic-update-slice_fusion
  43.4 30.2 %collective-permute-done.3 = bf16[256,1536]{1,0:T(8,128)(2,1)S(1)} collective-permute-done((bf16[256,1536]{1,0:T(8,128)(2,1)S(1)}, bf16[256,1536]{1,0:T(8,128)(2,1)S(1)}, u32[]{:S(2)}, u32[]{:S(2)}) %collective-permute-start.3) | collective-permute-done | bytes 786464 | tf_op jit(solution)/shard_map/ppermute | solution.py:303
  73.6 11.6 %collective-permute-start.4 = (bf16[640,1536]{1,0:T(8,128)(2,1)S(1)}, bf16[640,1536]{1,0:T(8,128)(2,1)S(1)}, u32[]{:S(2)}, u32[]{:S(2)}) collective-permute-start(bf16[640,1536]{1,0:T(8,128)(2,1)S(1)} %constant_dynamic-update-slice_fusion), channel_id=1, source_target_pairs={{0,16},{1,17},{2,18},{3,19},{4,20},{5,21},{6,22},{7,23},{8,24},{9,... | collective-permute-start | bytes 5898248 | tf_op jit(solution)/shard_map/ppermute | solution.py:287
  85.3 0.1 pad_add_fusion.place
  85.4 21.4 %collective-permute-done.4.around_ref = bf16[640,1536]{1,0:T(8,128)(2,1)S(1)} collective-permute-done((bf16[640,1536]{1,0:T(8,128)(2,1)S(1)}, bf16[640,1536]{1,0:T(8,128)(2,1)S(1)}, u32[]{:S(2)}, u32[]{:S(2)}) %collective-permute-start.4) | collective-permute-done | bytes 1966112 | tf_op jit(solution)/shard_map/ppermute | solution.py:287
  106.8 1.9 %normed_window.1 = (bf16[560,1536]{1,0:T(8,128)(2,1)S(1)}, bf16[384,1536]{1,0:T(8,128)(2,1)S(1)}) custom-call(s32[2]{0:T(128)S(1)} %pad_add_fusion.place, s32[2,32]{1,0:T(2,128)S(1)} %copy-done.2, f32[96,1536]{1,0:T(8,128)S(1)} %bitcast.8, bf16[640,1536]{1,0:T(8,128)(2,1)S(1)} %collective-permute-done.4.around_ref), custom_call_target="tpu_custom_call" | custom-call | flops 10000000 | bytes 4000000 | tf_op jit(solution)/shard_map/normed_window/pallas_call | solution.py:211
  108.7 15.6 %all-gather.2.cloned.1.call-done = bf16[3072,2304]{1,0:T(8,128)(2,1)} async-done(((bf16[192,2304]{1,0:T(8,128)(2,1)}), bf16[3072,2304]{1,0:T(8,128)(2,1)}) %all-gather.2.cloned.1.call-update) | async-done | bytes 14155792 | tf_op jit(solution)/shard_map/all_gather | solution.py:300
  124.3 19.1 %two_steps.1 = bf16[112,1536]{1,0:T(8,128)(2,1)} custom-call(s32[2]{0:T(128)S(1)} %pad_add_fusion.place, s32[2,32]{1,0:T(2,128)S(1)} %copy-done.2, s32[1,2]{1,0:T(1,128)S(1)} %copy-done.1, f32[96,1536]{1,0:T(8,128)S(1)} %bitcast.9, bf16[560,1536]{1,0:T(8,128)(2,1)S(1)} %get-tuple-element.16.normed_ref, bf16[384,1536]{1,0:T(8,128)(2,1)S(1)} %get-tuple-element.17.window_ref, ...), custom_call_target="tpu_custom_call" | custom-call | flops 12000000000 | bytes 20000000 | tf_op jit(solution)/shard_map/two_steps/pallas_call | solution.py:229
  (26 shorter events, 0.3 us)
Async XLA Ops:
  6.5 15.7 %copy-start.4 = (bf16[112,1536]{1,0:T(8,128)(2,1)S(1)}, bf16[112,1536]{1,0:T(8,128)(2,1)}, u32[]{:S(2)}) copy-start(bf16[112,1536]{1,0:T(8,128)(2,1)} %param.10) | copy-start | bytes 1032196
  6.5 15.7 %copy-start.3 = (bf16[112,1536]{1,0:T(8,128)(2,1)S(1)}, bf16[112,1536]{1,0:T(8,128)(2,1)}, u32[]{:S(2)}) copy-start(bf16[112,1536]{1,0:T(8,128)(2,1)} %param.11) | copy-start | bytes 1032196
  6.5 13.8 %copy-start.1 = (s32[1,2]{1,0:T(1,128)S(1)}, s32[1,2]{1,0:T(1,128)}, u32[]{:S(2)}) copy-start(s32[1,2]{1,0:T(1,128)} %bounds) | copy-start | bytes 28
  6.5 117.8 %all-gather.2.cloned.1.call-start = ((), (), s32[]{:S(2)}) async-start(), calls=%async_computation | async-start | bytes 15040512 | tf_op jit(solution)/shard_map/all_gather | solution.py:300
  8.8 22.1 %collective-permute-start.2 = (bf16[96,1152]{1,0:T(8,128)(2,1)S(1)}, bf16[96,1152]{1,0:T(8,128)(2,1)S(1)}, u32[]{:S(2)}, u32[]{:S(2)}) collective-permute-start(bf16[96,1152]{1,0:T(8,128)(2,1)S(1)} %constant_dynamic-slice_fusion), channel_id=1, source_target_pairs={{0,385},{1,384},{128,257},{129,256},{256,129},{257,128},{384,1},{3... | collective-permute-start | bytes 663560 | tf_op jit(solution)/shard_map/ppermute | solution.py:272
  22.5 15.8 %collective-permute-start = (bf16[128,1536]{1,0:T(8,128)(2,1)S(1)}, bf16[128,1536]{1,0:T(8,128)(2,1)S(1)}, u32[]{:S(2)}, u32[]{:S(2)}) collective-permute-start(bf16[128,1536]{1,0:T(8,128)(2,1)S(1)} %get-tuple-element.26), channel_id=1, source_target_pairs={{0,2},{1,3},{2,4},{3,5},{4,6},{5,7},{6,8},{7,9},{8,10},{9,11},{10,... | collective-permute-start | bytes 1179656 | tf_op jit(solution)/shard_map/ppermute | solution.py:287
  25.7 12.6 %collective-permute-start.1 = (bf16[128,1536]{1,0:T(8,128)(2,1)S(1)}, bf16[128,1536]{1,0:T(8,128)(2,1)S(1)}, u32[]{:S(2)}, u32[]{:S(2)}) collective-permute-start(bf16[128,1536]{1,0:T(8,128)(2,1)S(1)} %get-tuple-element.25), channel_id=1, source_target_pairs={{0,510},{1,511},{2,0},{3,1},{4,2},{5,3},{6,4},{7,5},{8,6},{9,7},{1... | collective-permute-start | bytes 1179656 | tf_op jit(solution)/shard_map/ppermute | solution.py:287
  30.9 7.3 %collective-permute-start.5 = (bf16[96,1152]{1,0:T(8,128)(2,1)S(1)}, bf16[96,1152]{1,0:T(8,128)(2,1)S(1)}, u32[]{:S(2)}, u32[]{:S(2)}) collective-permute-start(bf16[96,1152]{1,0:T(8,128)(2,1)S(1)} %collective-permute-done.2), channel_id=1, source_target_pairs={{0,32},{32,64},{64,96},{96,0},{48,16},{80,48},{112,80},{16,112},{1... | collective-permute-start | bytes 663560 | tf_op jit(solution)/shard_map/ppermute | solution.py:275
  39.7 45.6 %copy-start.5 = (f32[1536]{0:T(1024)S(1)}, f32[1536]{0:T(1024)}, u32[]{:S(2)}) copy-start(f32[1536]{0:T(1024)} %param.18) | copy-start | bytes 18436
  39.7 45.6 %copy-start.6 = (f32[1536]{0:T(1024)S(1)}, f32[1536]{0:T(1024)}, u32[]{:S(2)}) copy-start(f32[1536]{0:T(1024)} %param.19) | copy-start | bytes 18436
  39.7 67.1 %copy-start = (f32[32,3,1536]{2,0,1:T(8,128)S(1)}, f32[32,3,1536]{2,0,1:T(8,128)}, u32[]{:S(2)}) copy-start(f32[32,3,1536]{2,0,1:T(8,128)} %param.14) | copy-start | bytes 1769476
  39.7 67.1 %copy-start.2 = (s32[2,32]{1,0:T(2,128)S(1)}, s32[2,32]{1,0:T(2,128)}, u32[]{:S(2)}) copy-start(s32[2,32]{1,0:T(2,128)} %levels.3) | copy-start | bytes 772
  39.8 33.8 %collective-permute-start.3 = (bf16[256,1536]{1,0:T(8,128)(2,1)S(1)}, bf16[256,1536]{1,0:T(8,128)(2,1)S(1)}, u32[]{:S(2)}, u32[]{:S(2)}) collective-permute-start(bf16[256,1536]{1,0:T(8,128)(2,1)S(1)} %pad_maximum_fusion), channel_id=1, source_target_pairs={{0,1},{1,0},{2,3},{3,2},{4,5},{5,4},{6,7},{7,6},{8,9},{9,8},{10,11... | collective-permute-start | bytes 2359304 | tf_op jit(solution)/shard_map/ppermute | solution.py:303
  73.6 33.2 %collective-permute-start.4 = (bf16[640,1536]{1,0:T(8,128)(2,1)S(1)}, bf16[640,1536]{1,0:T(8,128)(2,1)S(1)}, u32[]{:S(2)}, u32[]{:S(2)}) collective-permute-start(bf16[640,1536]{1,0:T(8,128)(2,1)S(1)} %constant_dynamic-update-slice_fusion), channel_id=1, source_target_pairs={{0,16},{1,17},{2,18},{3,19},{4,20},{5,21},{6,22},{7,23},{8,24},{9,... | collective-permute-start | bytes 5898248 | tf_op jit(solution)/shard_map/ppermute | solution.py:287
Sparse Core Ops, SparseCore 0:
  39.6 84.6 all-gather.1
